TPU v7x, 32 devices: a whole 2x2x4 slice. The times are simulated.
32 devices in a mesh: sec: 4 (over x, core), blk: 4 (over z), aux: 2 (over y).
Axes of the slice: x: 2, y: 2, z: 4, core: 2. Of those that a mesh axis runs over, the one named last changes fastest.
Arguments:
- half_ints: bfloat16 [16, 2048, 1024], P('blk', 'aux', 'sec'), may hold values from -0.59765625 to 0.59765625
- coeffs: bfloat16 [1024, 1024], replicated, may hold values from -0.1875 to 0.1875
- occ_energy: float32 [16], replicated, may hold values from -1.5 to -0.3
- vir_energy: float32 [1024], replicated, may hold values from 0.2 to 3
Outputs:
- back_density: float32 [1024, 16, 2048], P('sec', 'blk', 'aux')
All inputs are finite; a program needn't handle non-finite values.
Results may differ from a plain program's by a relative error of at most 0.003.
Values may be sent and summed in bfloat16 or wider, within the bound.
A program may use at most 128 MiB of HBM per device.

v0:
```python
import jax
import jax.numpy as jnp
from jax import lax
from jax.sharding import PartitionSpec as P


def passed_along(x, axis, by):
    peers = lax.axis_size(axis)
    return lax.ppermute(x, axis, [(i, (i + by) % peers) for i in range(peers)])


def shards(half_ints, coeffs, occ_energy, vir_energy):
    sec_index = lax.axis_index("sec")
    blk_index = lax.axis_index("blk")
    aux_index = lax.axis_index("aux")
    cycle_size = lax.axis_size("blk")
    sec_count = lax.axis_size("sec")
    occ_block = half_ints.shape[0]
    aux_half = half_ints.shape[1]
    basis_slice = half_ints.shape[2]
    vir_total = coeffs.shape[1]
    vir_slice = vir_total // sec_count
    segment = lax.all_gather(half_ints, "sec", axis=2, tiled=True)
    width_here = segment.shape[2]
    flattened = segment.reshape(occ_block * aux_half, width_here)
    summed = jnp.dot(flattened, coeffs, preferred_element_type=jnp.float32)
    transformed = summed.astype(jnp.bfloat16).reshape(occ_block, aux_half, vir_total)
    home_block = lax.all_gather(transformed, "aux", axis=1, tiled=True)
    own_rows = lax.dynamic_slice_in_dim(home_block, sec_index * vir_slice, vir_slice, 2)
    own_energy = lax.dynamic_slice_in_dim(occ_energy, blk_index * occ_block, occ_block)
    own_virtual = lax.dynamic_slice_in_dim(vir_energy, sec_index * vir_slice, vir_slice)

    def pair_step(totals, visiting, cycle_step):
        source = (blk_index - cycle_step) % cycle_size
        visit_energy = lax.dynamic_slice_in_dim(occ_energy, source * occ_block, occ_block)
        integral_tiles = jnp.einsum(
            "ipa,jpb->iajb", own_rows, visiting, preferred_element_type=jnp.float32
        )
        denominator = (
            own_energy[:, None, None, None]
            + visit_energy[None, None, :, None]
            - own_virtual[None, :, None, None]
            - vir_energy[None, None, None, :]
        )
        amplitude = (1.3 * integral_tiles / denominator).astype(jnp.bfloat16)
        return totals + jnp.einsum(
            "iajb,jpb->ipa", amplitude, visiting, preferred_element_type=jnp.float32
        )

    start_totals = jnp.zeros(own_rows.shape, jnp.float32)
    half_cycle = cycle_size // 2
    shifted = passed_along(home_block, "blk", 1)
    visiting = jnp.where(aux_index == 1, shifted, home_block)

    def turn_body(turn_index, carry):
        totals, current = carry
        totals = pair_step(totals, current, 2 * turn_index + aux_index)
        current = passed_along(current, "blk", 2)
        return (totals, current)

    totals, visiting = lax.fori_loop(0, half_cycle - 1, turn_body, (start_totals, visiting))
    totals = pair_step(totals, visiting, cycle_size - 2 + aux_index)
    density = lax.psum_scatter(totals, "aux", scatter_dimension=1, tiled=True)
    density_half = density.astype(jnp.bfloat16)
    wide_density = lax.all_gather(density_half, "sec", axis=2, tiled=True)
    coeff_rows = lax.dynamic_slice_in_dim(coeffs, sec_index * basis_slice, basis_slice, 0)
    result = jnp.einsum("ma,ipa->mip", coeff_rows, wide_density, preferred_element_type=jnp.float32)
    return result


def solution(mesh):
    placed = (P("blk", "aux", "sec"), P(), P(), P())
    return jax.shard_map(
        shards, mesh=mesh, in_specs=placed, out_specs=P("sec", "blk", "aux"), check_vma=False
    )
```

profile of v0, /device:TPU:1, one launch (start us, length us, event | category | flops | bytes accessed | tf_op | source)
XLA Modules:
  0.0 1688.4 jit_solution(6386816307208011693)
XLA Ops:
  6.5 0.0 copy-start
  6.5 0.0 all-gather.4.cloned.1.call-start
  6.5 0.7 all-gather.4.cloned.1.call-update
  7.3 0.0 all-gather.6.cloned.1.call-start
  7.3 63.5 %all-gather.4.cloned.1.call-done = bf16[4,1024,1024]{2,1,0:T(8,128)(2,1)} async-done(((bf16[4,1024,256]{2,1,0:T(8,128)(2,1)}), bf16[4,1024,1024]{2,1,0:T(8,128)(2,1)}) %all-gather.4.cloned.1.call-update) | async-done | bytes 8388624 | tf_op jit(solution)/shard_map/all_gather | solution.py:23
  70.9 0.0 copy-done
  70.9 14.6 convolution_convert_fusion
  85.4 0.0 all-gather.6.cloned.1.call-update
  85.4 0.0 reduce-scatter.2.cloned.1.call-start
  85.5 198.6 %all-gather.6.cloned.1.call-done = bf16[4,2048,1024]{2,1,0:T(8,128)(2,1)} async-done(((bf16[4,1024,1024]{2,1,0:T(8,128)(2,1)}), bf16[4,2048,1024]{2,1,0:T(8,128)(2,1)}) %all-gather.6.cloned.1.call-update) | async-done | bytes 16777232 | tf_op jit(solution)/shard_map/all_gather | solution.py:28
  284.0 1.4 collective-permute-start
  285.4 0.0 copy-start.1
  285.4 0.0 copy-start.2
  285.4 362.0 %collective-permute-done = bf16[4,2048,1024]{2,1,0:T(8,128)(2,1)} collective-permute-done((bf16[4,2048,1024]{2,1,0:T(8,128)(2,1)}, bf16[4,2048,1024]{2,1,0:T(8,128)(2,1)}, u32[]{:S(2)}, u32[]{:S(2)}) %collective-permute-start) | collective-permute-done | bytes 16777248 | tf_op jit(solution)/shard_map/ppermute | solution.py:9
  647.4 14.0 broadcast_select_fusion
  661.4 0.3 collective-permute-start.1
  661.7 0.0 copy-done.1
  661.7 0.1 dynamic_slice.23
  661.8 0.0 copy-done.2
  661.8 0.1 fusion.29
  661.9 0.1 broadcast_add_fusion
  662.0 0.1 broadcast_subtract_fusion
  662.1 25.2 %fusion.6 = f32[4,256,4,1024]{3,1,2,0:T(8,128)S(1)} fusion(bf16[4,2048,1024]{2,1,0:T(8,128)(2,1)} %broadcast_select_fusion, bf16[4,2048,1024]{2,1,0:T(8,128)(2,1)} %all-gather.6.cloned.1.call-done, s32[]{:T(128)S(6)} %select_n.36), kind=kOutput, calls=%fused_computation.6 | convolution fusion | flops 17179869184 | bytes 37748740 | tf_op jit(solution)/shard_map/while/body/eval_jaxpr/ipa,jpb->iajb/dot_general | solution.py:36
  687.3 696.1 %collective-permute-done.1 = bf16[4,2048,1024]{2,1,0:T(8,128)(2,1)} collective-permute-done((bf16[4,2048,1024]{2,1,0:T(8,128)(2,1)}, bf16[4,2048,1024]{2,1,0:T(8,128)(2,1)}, u32[]{:S(2)}, u32[]{:S(2)}) %collective-permute-start.1) | collective-permute-done | bytes 16777248 | tf_op jit(solution)/shard_map/while/body/eval_jaxpr/ppermute | solution.py:9
  1383.4 23.7 %fusion.2 = f32[4,256,4,1024]{3,1,2,0:T(8,128)} fusion(bf16[4,2048,1024]{2,1,0:T(8,128)(2,1)} %collective-permute-done.1, bf16[4,2048,1024]{2,1,0:T(8,128)(2,1)} %all-gather.6.cloned.1.call-done, s32[]{:T(128)S(6)} %select_n.36), kind=kOutput, calls=%fused_computation.2 | convolution fusion | flops 17179869184 | bytes 37748740 | tf_op jit(solution)/shard_map/ipa,jpb->iajb/dot_general | solution.py:36
  1407.2 43.9 %fusion.11 = (bf16[4,256,4,1024]{3,2,1,0:T(4,128)(2,1)S(1)}, bf16[4,256,4,1024]{3,2,1,0:T(4,128)(2,1)}) fusion(f32[4,256,4,1024]{3,1,2,0:T(8,128)} %fusion.2, f32[4,256,4]{2,1,0:T(8,128)S(1)} %get-tuple-element.27, f32[1024]{0:T(1024)S(1)} %copy-done.1, f32[4,256,4]{2,1,0:T(8,128)S(1)} %get-tuple-element.28, f32[4,256,4,1024]{3,1,2,0:T(8,128)S(1)} %fusion.6), kind=kLoop, calls=%fused_computation.13 | loop fusion | flops 33554432 | bytes 50368512 | tf_op jit(solution)/shard_map/convert_element_type | solution.py:45
  1451.1 29.3 %fusion.4 = f32[2048,4,256,1]{2,0,3,1:T(8,128)} fusion(bf16[4,2048,1024]{2,1,0:T(8,128)(2,1)} %broadcast_select_fusion, bf16[4,256,4,1024]{3,2,1,0:T(4,128)(2,1)} %get-tuple-element.26), kind=kOutput, calls=%fused_computation.4 | convolution fusion | flops 17179869184 | bytes 33554432 | tf_op jit(solution)/shard_map/while/body/eval_jaxpr/iajb,jpb->ipa/dot_general | solution.py:46
  1480.4 28.6 %fusion.12 = f32[4,2048,256]{2,1,0:T(8,128)} fusion(f32[2048,4,256,1]{2,0,3,1:T(8,128)} %fusion.4, bf16[4,256,4,1024]{3,2,1,0:T(4,128)(2,1)S(1)} %get-tuple-element.25, bf16[4,2048,1024]{2,1,0:T(8,128)(2,1)} %collective-permute-done.1), kind=kOutput, calls=%fused_computation.16 | convolution fusion | flops 17181966336 | bytes 41943040 | tf_op jit(solution)/shard_map/iajb,jpb->ipa/dot_general | solution.py:46
  1509.0 0.0 reduce-scatter.2.cloned.1.call-update
  1509.0 0.0 all-gather.8.cloned.1.call-start
  1509.1 98.2 %reduce-scatter.2.cloned.1.call-done = f32[4,1024,256]{2,1,0:T(8,128)} async-done(((f32[4,2048,256]{2,1,0:T(8,128)}), f32[4,1024,256]{2,1,0:T(8,128)}) %reduce-scatter.2.cloned.1.call-update) | async-done | bytes 4194320 | tf_op jit(solution)/shard_map/reduce_scatter | solution.py:63
  1607.3 3.7 convert_element_type.16
  1611.0 0.0 all-gather.8.cloned.1.call-update
  1611.0 60.0 %all-gather.8.cloned.1.call-done = bf16[4,1024,1024]{2,1,0:T(8,128)(2,1)} async-done(((bf16[4,1024,256]{2,1,0:T(8,128)(2,1)}), bf16[4,1024,1024]{2,1,0:T(8,128)(2,1)}) %all-gather.8.cloned.1.call-update) | async-done | bytes 8388624 | tf_op jit(solution)/shard_map/all_gather | solution.py:65
  1671.0 5.7 fusion.23
  1676.8 4.7 copy.5
Async XLA Ops:
  6.5 64.3 %copy-start = (bf16[1024,1024]{1,0:T(8,128)(2,1)S(1)}, bf16[1024,1024]{1,0:T(8,128)(2,1)}, u32[]{:S(2)}) copy-start(bf16[1024,1024]{1,0:T(8,128)(2,1)} %param.5) | copy-start | bytes 6291460
  6.5 64.3 %all-gather.4.cloned.1.call-start = ((), (), s32[]{:S(2)}) async-start(), calls=%async_computation.1 | async-start | bytes 10485760 | tf_op jit(solution)/shard_map/all_gather | solution.py:23
  7.3 276.8 %all-gather.6.cloned.1.call-start = ((), (), s32[]{:S(2)}) async-start(), calls=%async_computation.2 | async-start | bytes 25165824 | tf_op jit(solution)/shard_map/all_gather | solution.py:28
  85.4 1521.9 %reduce-scatter.2.cloned.1.call-start = ((), (), s32[]{:S(2)}) async-start(), calls=%async_computation.3 | async-start | bytes 12582912 | tf_op jit(solution)/shard_map/reduce_scatter | solution.py:63
  284.0 363.4 %collective-permute-start = (bf16[4,2048,1024]{2,1,0:T(8,128)(2,1)}, bf16[4,2048,1024]{2,1,0:T(8,128)(2,1)}, u32[]{:S(2)}, u32[]{:S(2)}) collective-permute-start(bf16[4,2048,1024]{2,1,0:T(8,128)(2,1)} %all-gather.6.cloned.1.call-done), channel_id=1, source_target_pairs={{0,2},{2,4},{4,6},{6,0},{1,3},{3,5},{5,7},{7,1},{8,10},{10,12},{12... | collective-permute-start | bytes 50331656 | tf_op jit(solution)/shard_map/ppermute | solution.py:9
  285.4 376.4 %copy-start.1 = (f32[1024]{0:T(1024)S(1)}, f32[1024]{0:T(1024)}, u32[]{:S(2)}) copy-start(f32[1024]{0:T(1024)} %param.7) | copy-start | bytes 12292
  285.4 376.4 %copy-start.2 = (f32[16]{0:T(128)S(1)}, f32[16]{0:T(128)}, u32[]{:S(2)}) copy-start(f32[16]{0:T(128)} %param.6) | copy-start | bytes 196
  661.4 722.0 %collective-permute-start.1 = (bf16[4,2048,1024]{2,1,0:T(8,128)(2,1)}, bf16[4,2048,1024]{2,1,0:T(8,128)(2,1)}, u32[]{:S(2)}, u32[]{:S(2)}) collective-permute-start(bf16[4,2048,1024]{2,1,0:T(8,128)(2,1)} %broadcast_select_fusion), channel_id=1, source_target_pairs={{0,4},{2,6},{4,0},{6,2},{1,5},{3,7},{5,1},{7,3},{8,12},{10,14},{12... | collective-permute-start | bytes 50331656 | tf_op jit(solution)/shard_map/while/body/eval_jaxpr/ppermute | solution.py:9
  1509.0 162.0 %all-gather.8.cloned.1.call-start = ((), (), s32[]{:S(2)}) async-start(), calls=%async_computation.4 | async-start | bytes 10485760 | tf_op jit(solution)/shard_map/all_gather | solution.py:65
Sparse Core Ops, SparseCore 0:
  8.9 61.8 all-gather.3
  85.6 198.4 all-gather.5
  1509.1 98.1 reduce-scatter.1
  1611.2 59.8 all-gather.7
where the time goes:
time: 1690 us
  waiting for transfers between devices  1480 us (88%)
  matrix products  127 us (8%)
  other arithmetic  61.9 us (4%)
    ppermute x2, waiting for transfers between devices, passed_along(): return lax.ppermute(x, axis, [(i, (i + by) % peers) for i in range(peers)])  1060 us
    all_gather x1, waiting for transfers between devices, shards(): home_block = lax.all_gather(transformed, 'aux', axis=1, tiled=True)  199 us
    reduce_scatter x1, waiting for transfers between devices, shards(): density = lax.psum_scatter(totals, 'aux', scatter_dimension=1, tiled=True)  98.2 us
    all_gather x1, waiting for transfers between devices, shards(): segment = lax.all_gather(half_ints, 'sec', axis=2, tiled=True)  63.5 us
    all_gather x1, waiting for transfers between devices, shards(): wide_density = lax.all_gather(density_half, 'sec', axis=2, tiled=True)  60 us
    dot_general x2, matrix products, pair_step(): jnp.einsum('iajb,jpb->ipa', amplitude, visiting, preferred_element_type=j...  57.9 us
    dot_general x2, matrix products, pair_step(): jnp.einsum('ipa,jpb->iajb', own_rows, visiting, preferred_element_type=jn...  48.9 us
    convert_element_type x1, other arithmetic, pair_step(): amplitude = (1.3 * integral_tiles / denominator).astype(jnp.bfloat16)  43.9 us
  transfers between devices with their start and end apart: 6, of which 6 were waited for; matrix products, arithmetic and copies ran while one was open for 2% of the time, Pallas kernels for 0%

commit v1 on v0

v1 whole, which is shorter than its diff:
```python
import jax
import jax.numpy as jnp
from jax import lax
from jax.sharding import PartitionSpec as P

CORES = 2


def shards(half_ints, coeffs, occ_energy, vir_energy):
    sec_size, blk_size, aux_size = (lax.axis_size(n) for n in ("sec", "blk", "aux"))
    sec_index, blk_index, aux_index = (lax.axis_index(n) for n in ("sec", "blk", "aux"))
    cores = CORES if sec_size % CORES == 0 else 1
    xs = sec_size // cores
    x_index, core_index = sec_index // cores, sec_index % cores
    occ_block, aux_half, basis_slice = half_ints.shape
    vir_total = coeffs.shape[1]
    vir_part = vir_total // cores
    key_width = vir_part // (xs * aux_size)
    quarter = aux_half // xs
    aux_total = aux_half * aux_size

    def plane_shift(v, s, t):
        perm = []
        for i in range(sec_size):
            for j in range(aux_size):
                to = ((i // cores + s) % xs) * cores + i % cores
                perm.append((i * aux_size + j, to * aux_size + (j + t) % aux_size))
        return lax.ppermute(v, ("sec", "aux"), perm)

    def core_shift(v, k):
        perm = [(i, i // cores * cores + (i + k) % cores) for i in range(sec_size)]
        return lax.ppermute(v, "sec", perm)

    def gathered_cores(v, axis):
        return jnp.concatenate([v] + [core_shift(v, k) for k in range(1, cores)], axis)

    def line(v, by):
        perm = [(i, i + by) for i in range(blk_size) if 0 <= i + by < blk_size]
        return lax.ppermute(v, "blk", perm)

    pieces = []
    for s in range(xs):
        start = ((x_index + s) % xs) * quarter
        part = lax.dynamic_slice_in_dim(half_ints, start, quarter, 1)
        pieces.append(plane_shift(part, s, 0) if s else part)
    rows = gathered_cores(jnp.concatenate(pieces, 2), 2)
    own_columns = lax.dynamic_slice_in_dim(coeffs, core_index * vir_part, vir_part, 1)
    blocks = []
    for k in range(cores):
        for s in range(xs):
            source = ((x_index - s) % xs) * cores + (core_index - k) % cores
            blocks.append(lax.dynamic_slice_in_dim(own_columns, source * basis_slice, basis_slice, 0))
    transformed = jnp.einsum(
        "ipm,ma->ipa", rows, jnp.concatenate(blocks, 0), preferred_element_type=jnp.float32
    ).astype(jnp.bfloat16)

    def key_columns(s, t):
        group = ((x_index + s) % xs) * aux_size + (aux_index + t) % aux_size
        return lax.dynamic_slice_in_dim(transformed, group * key_width, key_width, 2)

    turns = [(t, s) for t in range(aux_size) for s in range(xs)]
    keys = [plane_shift(key_columns(s, t), s, t) if s or t else key_columns(0, 0) for t, s in turns]
    own_keys = jnp.concatenate(keys, 1)
    transformed, own_keys = lax.optimization_barrier((transformed, own_keys))
    queries = jnp.concatenate(
        [plane_shift(transformed, s, t) if s or t else transformed for t, s in turns], 1
    )

    up, down = [own_keys], [own_keys]
    for _ in range(blk_size - 1):
        up.append(line(up[-1], 1))
        down.append(line(down[-1], -1))

    def arrival(z, stage):
        others = sorted((b for b in range(blk_size)), key=lambda b: (abs(b - z), b))
        return others[stage]

    own_energy = lax.dynamic_slice_in_dim(occ_energy, blk_index * occ_block, occ_block)
    own_virtual = lax.dynamic_slice_in_dim(vir_energy, core_index * vir_part, vir_part)
    group = x_index * aux_size + aux_index
    key_virtual = jnp.concatenate([
        lax.dynamic_slice_in_dim(
            vir_energy, (core_index - k) % cores * vir_part + group * key_width, key_width
        )
        for k in range(cores)
    ])

    def stage_keys(stage):
        choices = {}
        for z in range(blk_size):
            b = arrival(z, stage)
            choices.setdefault(b - z, []).append(z)
        chosen = None
        for offset, planes in choices.items():
            block = down[offset] if offset > 0 else up[-offset]
            if chosen is None:
                chosen = block
            else:
                here = jnp.any(blk_index == jnp.array(planes))
                chosen = jnp.where(here, block, chosen)
        source = jnp.array([arrival(z, stage) for z in range(blk_size)])[blk_index]
        energy = lax.dynamic_slice_in_dim(occ_energy, source * occ_block, occ_block)
        return gathered_cores(chosen, 2), energy

    def pair_step(rows, energy_rows, visiting, visit_energy):
        tiles = jnp.einsum("ipa,jpb->iajb", rows, visiting, preferred_element_type=jnp.float32)
        denominator = (
            energy_rows[:, None, None, None]
            + visit_energy[None, None, :, None]
            - own_virtual[None, :, None, None]
            - key_virtual[None, None, None, :]
        )
        amplitude = (1.3 * tiles / denominator).astype(jnp.bfloat16)
        return jnp.einsum("iajb,jpb->ipa", amplitude, visiting, preferred_element_type=jnp.float32)

    totals = None
    for stage in range(blk_size - 1):
        visiting, visit_energy = stage_keys(stage)
        if totals is not None:
            totals, visiting = lax.optimization_barrier((totals, visiting))
        term = pair_step(queries, own_energy, visiting, visit_energy)
        totals = term if totals is None else totals + term
    visiting, visit_energy = stage_keys(blk_size - 1)
    wide = []
    for i in range(occ_block):
        part = pair_step(queries[i : i + 1], own_energy[i : i + 1], visiting, visit_energy)[0]
        if totals is not None:
            part = part + totals[i]
        part = part.reshape(aux_size, xs, quarter, vir_part)
        half = part[0]
        for t in range(1, aux_size):
            half = half + plane_shift(part[(-t) % aux_size].astype(jnp.bfloat16), 0, t)
        total = half
        for s in range(1, xs):
            received = plane_shift(half.astype(jnp.bfloat16), s, 0)
            total = total + jnp.roll(received, s, 0)
        whole = gathered_cores(total.astype(jnp.bfloat16), 2)
        wide.append(whole)
    wide = jnp.stack(wide)
    wide = jnp.concatenate(
        [lax.dynamic_slice_in_dim(wide, (x_index - p) % xs, 1, 1)[:, 0] for p in range(xs)], 1
    )
    coeff_rows = lax.dynamic_slice_in_dim(coeffs, sec_index * basis_slice, basis_slice, 0)
    coeff_rows = jnp.concatenate([
        lax.dynamic_slice_in_dim(coeff_rows, (core_index - k) % cores * vir_part, vir_part, 1)
        for k in range(cores)
    ], 1)
    return jnp.einsum("ma,ipa->mip", coeff_rows, wide, preferred_element_type=jnp.float32)


def solution(mesh):
    placed = (P("blk", "aux", "sec"), P(), P(), P())
    return jax.shard_map(
        shards, mesh=mesh, in_specs=placed, out_specs=P("sec", "blk", "aux"), check_vma=False
    )
```

time: 1690 us -> 526 us (0.31)
  waiting for transfers between devices: 1480 us -> 228 us
  starting transfers between devices: 1.81 us -> 53.3 us
  local copies, waits for them, and re-layouts: 4.87 us -> 40.4 us
    ppermute x2 -> x30, waiting for transfers between devices: 1060 us -> 228 us  [the longest x15 152 us: plane_shift(): return lax.ppermute(v, ('sec', 'aux'), perm)]
    all_gather x3 -> x0, waiting for transfers between devices: 322 us -> none  [the longest x1 199 us: shards(): home_block = lax.all_gather(transformed, 'aux', axis=1, tiled=True)]
    reduce_scatter x1 -> x0, waiting for transfers between devices: 98.2 us -> none  [shards(): density = lax.psum_scatter(totals, 'aux', scatter_dimension=1, tiled=True)]
    ppermute x2 -> x30, starting transfers between devices: 1.68 us -> 53.3 us  [the longest x9 20.8 us: core_shift(): return lax.ppermute(v, 'sec', perm)]
    dot_general x2 -> x7, matrix products: 57.9 us -> 106 us  [pair_step(): jnp.einsum('iajb,jpb->ipa', amplitude, visiting, preferred_element_type=j...]
    convert_element_type x2 -> x8, other arithmetic: 47.7 us -> 4.17 us  [the longest x4 2.73 us: shards(): whole = gathered_cores(total.astype(jnp.bfloat16), 2)]
    dot_general x4, matrix products: 69.2 us -> 35.3 us  [the longest x2 26.6 us: pair_step(): jnp.einsum('ipa,jpb->iajb', rows, visiting, preferred_element_type=jnp.fl...]
    add x1 -> x5, other arithmetic: 0.07 us -> 27.6 us  [the longest x2 24.8 us: shards(): totals = term if totals is None else totals + term]
  transfers between devices with their start and end apart: 6 -> 30, of which waited for: 6 -> 11; matrix products, arithmetic and copies ran while one was open for 2% -> 37% of each run, Pallas kernels for 0% -> 0%
where the time goes in v1:
time: 526 us; the launch traced here: 519 us
  waiting for transfers between devices  228 us (43%)
  matrix products  142 us (27%)
  starting transfers between devices  53.3 us (10%)
  other arithmetic  52.6 us (10%)
  local copies, waits for them, and re-layouts  40.4 us (8%)
    ppermute x15, waiting for transfers between devices, plane_shift(): return lax.ppermute(v, ('sec', 'aux'), perm)  152 us
    dot_general x7, matrix products, pair_step(): jnp.einsum('iajb,jpb->ipa', amplitude, visiting, preferred_element_type=j...  106 us
    ppermute x6, waiting for transfers between devices, line(): return lax.ppermute(v, 'blk', perm)  75.6 us
    dot_general x2, matrix products, pair_step(): jnp.einsum('ipa,jpb->iajb', rows, visiting, preferred_element_type=jnp.fl...  26.6 us
    add x2, other arithmetic, shards(): totals = term if totals is None else totals + term  24.8 us
    ppermute x9, starting transfers between devices, core_shift(): return lax.ppermute(v, 'sec', perm)  20.8 us
    ppermute x6, starting transfers between devices, line(): return lax.ppermute(v, 'blk', perm)  19.8 us
    ppermute x15, starting transfers between devices, plane_shift(): return lax.ppermute(v, ('sec', 'aux'), perm)  12.8 us
  transfers between devices with their start and end apart: 30, of which 11 were waited for; matrix products, arithmetic and copies ran while one was open for 37% of the time, Pallas kernels for 0%

profile of v1, /device:TPU:1, one launch (start us, length us, event | category | flops | bytes accessed | tf_op | source)
XLA Modules:
  0.0 519.1 jit_solution(1532666015535647318)
XLA Ops:
  1.7 2.1 collective-permute-start
  3.8 22.9 %collective-permute-done = bf16[4,512,256]{2,1,0:T(8,128)(2,1)S(1)} collective-permute-done((bf16[4,512,256]{2,1,0:T(8,128)(2,1)S(1)}, bf16[4,512,256]{2,1,0:T(8,128)(2,1)S(1)}, u32[]{:S(2)}, u32[]{:S(2)}) %collective-permute-start) | collective-permute-done | bytes 1048608 | tf_op jit(solution)/shard_map/ppermute | solution.py:28
  29.1 3.3 fusion.69
  33.0 4.2 fusion.39
  37.7 2.5 collective-permute-start.4
  40.6 11.4 %collective-permute-done.4 = bf16[4,512,128]{2,1,0:T(8,128)(2,1)S(1)} collective-permute-done((bf16[4,512,128]{2,1,0:T(8,128)(2,1)S(1)}, bf16[4,512,128]{2,1,0:T(8,128)(2,1)S(1)}, u32[]{:S(2)}, u32[]{:S(2)}) %collective-permute-start.4) | collective-permute-done | bytes 524320 | tf_op jit(solution)/shard_map/ppermute | solution.py:28
  52.0 11.8 %collective-permute-done.3 = bf16[4,512,128]{2,1,0:T(8,128)(2,1)S(1)} collective-permute-done((bf16[4,512,128]{2,1,0:T(8,128)(2,1)S(1)}, bf16[4,512,128]{2,1,0:T(8,128)(2,1)S(1)}, u32[]{:S(2)}, u32[]{:S(2)}) %collective-permute-start.3) | collective-permute-done | bytes 524320 | tf_op jit(solution)/shard_map/ppermute | solution.py:28
  64.0 4.8 collective-permute-start.5
  70.0 41.7 %collective-permute-done.5 = bf16[4,2048,128]{2,1,0:T(8,128)(2,1)} collective-permute-done((bf16[4,2048,128]{2,1,0:T(8,128)(2,1)S(1)}, bf16[4,2048,128]{2,1,0:T(8,128)(2,1)}, u32[]{:S(2)}, u32[]{:S(2)}) %collective-permute-start.5) | collective-permute-done | bytes 2097184 | tf_op jit(solution)/shard_map/ppermute | solution.py:39
  111.7 5.6 %collective-permute-start.6 = (bf16[4,2048,128]{2,1,0:T(8,128)(2,1)}, bf16[4,2048,128]{2,1,0:T(8,128)(2,1)}, u32[]{:S(2)}, u32[]{:S(2)}) collective-permute-start(bf16[4,2048,128]{2,1,0:T(8,128)(2,1)} %collective-permute-done.5), channel_id=1, source_target_pairs={{0,2},{2,4},{4,6},{1,3},{3,5},{5,7},{8,10},{10,12},{12,14},{9,11},... | collective-permute-start | bytes 6291464 | tf_op jit(solution)/shard_map/ppermute | solution.py:39
  125.9 33.8 %collective-permute-done.6 = bf16[4,2048,128]{2,1,0:T(8,128)(2,1)} collective-permute-done((bf16[4,2048,128]{2,1,0:T(8,128)(2,1)}, bf16[4,2048,128]{2,1,0:T(8,128)(2,1)}, u32[]{:S(2)}, u32[]{:S(2)}) %collective-permute-start.6) | collective-permute-done | bytes 2097184 | tf_op jit(solution)/shard_map/ppermute | solution.py:39
  159.7 5.4 %collective-permute-start.7 = (bf16[4,2048,128]{2,1,0:T(8,128)(2,1)}, bf16[4,2048,128]{2,1,0:T(8,128)(2,1)}, u32[]{:S(2)}, u32[]{:S(2)}) collective-permute-start(bf16[4,2048,128]{2,1,0:T(8,128)(2,1)} %collective-permute-done.6), channel_id=1, source_target_pairs={{0,2},{2,4},{4,6},{1,3},{3,5},{5,7},{8,10},{10,12},{12,14},{9,11},... | collective-permute-start | bytes 6291464 | tf_op jit(solution)/shard_map/ppermute | solution.py:39
  168.8 1.9 broadcast_add_fusion.5
  170.7 2.7 collective-permute-start.15
  174.4 1.7 constant_dynamic-update-slice_fusion.2
  176.1 1.7 constant_dynamic-update-slice_fusion.1
  177.9 32.5 %collective-permute-done.14 = bf16[4,512,512]{2,1,0:T(8,128)(2,1)} collective-permute-done((bf16[4,512,512]{2,1,0:T(8,128)(2,1)S(1)}, bf16[4,512,512]{2,1,0:T(8,128)(2,1)}, u32[]{:S(2)}, u32[]{:S(2)}) %collective-permute-start.14) | collective-permute-done | bytes 2097184 | tf_op jit(solution)/shard_map/ppermute | solution.py:28
  212.1 3.2 copy-done.7
  215.3 6.3 %select_select_fusion.1 = (bf16[4,2048,128]{2,1,0:T(8,128)(2,1)}, bf16[4,2048,128]{2,1,0:T(8,128)(2,1)S(1)}, bf16[4,2048,128]{2,1,0:T(8,128)(2,1)}) fusion(bf16[4,2048,128]{2,1,0:T(8,128)(2,1)} %collective-permute-done.7, bf16[4,2048,128]{2,1,0:T(8,128)(2,1)} %collective-permute-done.6, bf16[4,2048,128]{2,1,0:T(8,128)(2,1)} %collective-permute-done.9, ...), kind=kLoop, calls=%fused_computation.83 | loop fusion | flops 6291456 | bytes 18874372 | tf_op jit(solution)/shard_map/jit(_where)/select_n | solution.py:100
  221.6 4.4 collective-permute-start.16
  226.0 27.7 %convolution_bitcast_fusion = f32[4,2048,512]{2,1,0:T(8,128)} fusion(f32[256]{0:T(256)S(1)} %pad_maximum_fusion.6, f32[4,512,4]{1,2,0:T(4,128)S(1)} %get-tuple-element.52, bf16[4,2048,128]{2,1,0:T(8,128)(2,1)} %collective-permute-done.15, bf16[4,2048,128]{2,1,0:T(8,128)(2,1)} %copy-done.5, bf16[4,2048,512]{2,1,0:T(8,128)(2,1)} %copy-done.7), kind=kOutput, calls=%fused_computation.16 | convolution fusion | flops 17205035008 | bytes 29393920 | tf_op jit(solution)/shard_map/iajb,jpb->ipa/dot_general | solution.py:114
  254.2 2.9 pad_maximum_fusion.2
  258.4 11.6 %fusion.6 = f32[4,512,4,256]{3,1,2,0:T(8,128)} fusion(bf16[4,2048,512]{2,1,0:T(8,128)(2,1)S(1)} %copy-done.8, bf16[4,2048,256]{2,1,0:T(8,128)(2,1)S(1)} %pad_maximum_fusion.2), kind=kOutput, calls=%fused_computation.9 | convolution fusion | flops 8589934592 | bytes 20971520 | tf_op jit(solution)/shard_map/ipa,jpb->iajb/dot_general | solution.py:106
  270.0 15.2 %fusion.10 = f32[2048,4,512,1]{2,0,3,1:T(8,128)} fusion(f32[4,512,4,256]{3,1,2,0:T(8,128)} %fusion.6, bf16[4,2048,256]{2,1,0:T(8,128)(2,1)S(1)} %pad_maximum_fusion.2, f32[4,512,4]{1,2,0:T(4,128)S(1)} %get-tuple-element.51, f32[256]{0:T(256)S(1)} %pad_maximum_fusion.6), kind=kOutput, calls=%fused_computation.17 | convolution fusion | flops 8598323200 | bytes 29393920 | tf_op jit(solution)/shard_map/iajb,jpb->ipa/dot_general | solution.py:114
  285.2 11.9 %bitcast_add_fusion.1 = f32[4,2048,512]{2,1,0:T(8,128)S(1)} fusion(f32[4,2048,512]{2,1,0:T(8,128)} %convolution_bitcast_fusion, f32[2048,4,512,1]{2,0,3,1:T(8,128)} %fusion.10), kind=kLoop, calls=%fused_computation.1 | loop fusion | flops 4194304 | bytes 50331648 | tf_op jit(solution)/shard_map/add | solution.py:122
  297.1 2.0 pad_maximum_fusion.3
  299.2 15.0 %fusion.4 = f32[4,512,4,256]{3,1,2,0:T(8,128)} fusion(bf16[4,2048,512]{2,1,0:T(8,128)(2,1)} %copy-done.7, bf16[4,2048,256]{2,1,0:T(8,128)(2,1)S(1)} %pad_maximum_fusion.3), kind=kOutput, calls=%fused_computation.7 | convolution fusion | flops 8589934592 | bytes 20971520 | tf_op jit(solution)/shard_map/ipa,jpb->iajb/dot_general | solution.py:106
  314.2 16.2 %fusion.11 = f32[2048,4,512,1]{2,0,3,1:T(8,128)} fusion(f32[4,512,4,256]{3,1,2,0:T(8,128)} %fusion.4, bf16[4,2048,256]{2,1,0:T(8,128)(2,1)} %copy-done, f32[4,512,4]{1,2,0:T(4,128)S(1)} %get-tuple-element.50, f32[256]{0:T(256)S(1)} %pad_maximum_fusion.6), kind=kOutput, calls=%fused_computation.18 | convolution fusion | flops 8598323200 | bytes 29393920 | tf_op jit(solution)/shard_map/iajb,jpb->ipa/dot_general | solution.py:114
  330.4 12.9 %bitcast_add_fusion = f32[4,2048,512]{2,1,0:T(8,128)} fusion(f32[4,2048,512]{2,1,0:T(8,128)S(1)} %bitcast_add_fusion.1, f32[2048,4,512,1]{2,0,3,1:T(8,128)} %fusion.11), kind=kLoop, calls=%fused_computation | loop fusion | flops 4194304 | bytes 50331648 | tf_op jit(solution)/shard_map/add | solution.py:122
  343.4 10.7 %fusion.12 = f32[2048,512]{1,0:T(8,128)} fusion(f32[4,2048,512]{2,1,0:T(8,128)} %bitcast_add_fusion, bf16[4,2048,512]{2,1,0:T(8,128)(2,1)} %copy-done.7, f32[512,4]{0,1:T(4,128)S(1)} %copy-done.15, f32[256]{0:T(256)S(1)} %pad_maximum_fusion.6, bf16[4,2048,128]{2,1,0:T(8,128)(2,1)} %collective-permute-done.11, bf16[4,2048,128]{2,1,0:T(8,128)(2,1)S(1)} %copy-done.4), kind=kOutput, calls=%fused_computation.20 | convolution fusion | flops 4314890240 | bytes 18883584 | tf_op jit(solution)/shard_map/iajb,jpb->ipa/dot_general | solution.py:114
  354.1 2.7 slice.190
  357.1 11.8 %fusion.13 = f32[2048,512]{1,0:T(8,128)} fusion(f32[4,2048,512]{2,1,0:T(8,128)} %bitcast_add_fusion, bf16[4,2048,512]{2,1,0:T(8,128)(2,1)} %copy-done.7, f32[512,4]{0,1:T(4,128)S(1)} %copy-done.14, f32[256]{0:T(256)S(1)} %pad_maximum_fusion.6, bf16[4,2048,128]{2,1,0:T(8,128)(2,1)} %collective-permute-done.11, bf16[4,2048,128]{2,1,0:T(8,128)(2,1)} %get-tuple-element.21), kind=kOutput, calls=%fused_computation.22 | convolution fusion | flops 4314890240 | bytes 18883584 | tf_op jit(solution)/shard_map/iajb,jpb->ipa/dot_general | solution.py:114
  368.9 2.7 slice.191
  372.8 12.3 %fusion.14 = f32[2048,512]{1,0:T(8,128)} fusion(f32[4,2048,512]{2,1,0:T(8,128)} %bitcast_add_fusion, bf16[4,2048,512]{2,1,0:T(8,128)(2,1)} %copy-done.7, f32[512,4]{0,1:T(4,128)S(1)} %copy-done.13, f32[256]{0:T(256)S(1)} %pad_maximum_fusion.6, bf16[4,2048,128]{2,1,0:T(8,128)(2,1)} %collective-permute-done.11, bf16[4,2048,128]{2,1,0:T(8,128)(2,1)} %get-tuple-element.21), kind=kOutput, calls=%fused_computation.24 | convolution fusion | flops 4314890240 | bytes 18883584 | tf_op jit(solution)/shard_map/iajb,jpb->ipa/dot_general | solution.py:114
  385.1 2.7 slice.192
  388.1 12.5 %fusion.15 = f32[2048,512]{1,0:T(8,128)} fusion(f32[4,2048,512]{2,1,0:T(8,128)} %bitcast_add_fusion, bf16[4,2048,512]{2,1,0:T(8,128)(2,1)} %copy-done.7, f32[256]{0:T(256)S(1)} %pad_maximum_fusion.6, f32[512,4]{0,1:T(4,128)S(1)} %copy-done.12, bf16[4,2048,128]{2,1,0:T(8,128)(2,1)} %collective-permute-done.11, bf16[4,2048,128]{2,1,0:T(8,128)(2,1)} %get-tuple-element.21), kind=kOutput, calls=%fused_computation.26 | convolution fusion | flops 4314890240 | bytes 18883584 | tf_op jit(solution)/shard_map/iajb,jpb->ipa/dot_general | solution.py:114
  400.6 1.9 slice.146
  409.1 17.1 %collective-permute-done.21 = bf16[2,512,512]{2,1,0:T(8,128)(2,1)S(1)} collective-permute-done((bf16[2,512,512]{2,1,0:T(8,128)(2,1)}, bf16[2,512,512]{2,1,0:T(8,128)(2,1)S(1)}, u32[]{:S(2)}, u32[]{:S(2)}) %collective-permute-start.21) | collective-permute-done | bytes 1048608 | tf_op jit(solution)/shard_map/ppermute | solution.py:28
  426.9 21.8 %collective-permute-done.18 = bf16[2,512,512]{2,1,0:T(8,128)(2,1)S(1)} collective-permute-done((bf16[2,512,512]{2,1,0:T(8,128)(2,1)S(1)}, bf16[2,512,512]{2,1,0:T(8,128)(2,1)S(1)}, u32[]{:S(2)}, u32[]{:S(2)}) %collective-permute-start.18) | collective-permute-done | bytes 1048608 | tf_op jit(solution)/shard_map/ppermute | solution.py:28
  453.0 3.0 collective-permute-start.26
  456.0 17.3 %collective-permute-done.22 = bf16[2,512,512]{2,1,0:T(8,128)(2,1)S(1)} collective-permute-done((bf16[2,512,512]{2,1,0:T(8,128)(2,1)S(1)}, bf16[2,512,512]{2,1,0:T(8,128)(2,1)S(1)}, u32[]{:S(2)}, u32[]{:S(2)}) %collective-permute-start.22) | collective-permute-done | bytes 1048608 | tf_op jit(solution)/shard_map/ppermute | solution.py:28
  473.8 4.7 collective-permute-start.23
  478.5 17.3 %collective-permute-done.19 = bf16[2,512,512]{2,1,0:T(8,128)(2,1)S(1)} collective-permute-done((bf16[2,512,512]{2,1,0:T(8,128)(2,1)S(1)}, bf16[2,512,512]{2,1,0:T(8,128)(2,1)S(1)}, u32[]{:S(2)}, u32[]{:S(2)}) %collective-permute-start.19) | collective-permute-done | bytes 1048608 | tf_op jit(solution)/shard_map/ppermute | solution.py:28
  496.3 2.6 collective-permute-start.20
  498.9 1.8 maximum_bitcast_fusion.6
  506.2 3.4 dynamic-slice_bitcast_fusion.1
  509.6 4.5 fusion
  514.1 4.7 copy.15
  (123 shorter events, 41.5 us)
Async XLA Ops:
  1.7 25.0 %collective-permute-start = (bf16[4,512,256]{2,1,0:T(8,128)(2,1)S(1)}, bf16[4,512,256]{2,1,0:T(8,128)(2,1)S(1)}, u32[]{:S(2)}, u32[]{:S(2)}) collective-permute-start(bf16[4,512,256]{2,1,0:T(8,128)(2,1)S(1)} %get-tuple-element.35), channel_id=1, source_target_pairs={{0,16},{1,17},{8,24},{9,25},{16,0},{17,1},{24,8},{25,9},{2,18},{3,... | collective-permute-start | bytes 3145736 | tf_op jit(solution)/shard_map/ppermute | solution.py:28
  27.8 5.2 %collective-permute-start.1 = (bf16[4,512,512]{2,1,0:T(8,128)(2,1)S(1)}, bf16[4,512,512]{2,1,0:T(8,128)(2,1)}, u32[]{:S(2)}, u32[]{:S(2)}) collective-permute-start(bf16[4,512,512]{2,1,0:T(8,128)(2,1)S(1)} %pad_maximum_fusion.4), channel_id=1, source_target_pairs={{0,8},{8,0},{16,24},{24,16},{1,9},{9,1},{17,25},{25,17},{2,10},{10... | collective-permute-start | bytes 6291464 | tf_op jit(solution)/shard_map/ppermute | solution.py:32
  37.2 84.1 %copy-start.21 = (s32[4]{0:T(128)S(1)}, s32[4]{0:T(128)}, u32[]{:S(2)}) copy-start(s32[4]{0:T(128)} %constant.209.clone) | copy-start | bytes 52
  37.3 85.3 %copy-start.20 = (s32[4]{0:T(128)S(1)}, s32[4]{0:T(128)}, u32[]{:S(2)}) copy-start(s32[4]{0:T(128)} %constant.206.clone) | copy-start | bytes 52
  37.3 86.6 %copy-start.19 = (s32[4]{0:T(128)S(1)}, s32[4]{0:T(128)}, u32[]{:S(2)}) copy-start(s32[4]{0:T(128)} %constant.203.clone) | copy-start | bytes 52
  37.3 87.9 %copy-start.11 = (f32[16]{0:T(128)S(1)}, f32[16]{0:T(128)}, u32[]{:S(2)}) copy-start(f32[16]{0:T(128)} %param.16) | copy-start | bytes 196
  37.3 88.0 %copy-start.18 = (s32[2]{0:T(128)S(1)}, s32[2]{0:T(128)}, u32[]{:S(2)}) copy-start(s32[2]{0:T(128)} %constant.204.clone) | copy-start | bytes 28
  37.3 129.3 %copy-start.16 = (f32[1024]{0:T(1024)S(1)}, f32[1024]{0:T(1024)}, u32[]{:S(2)}) copy-start(f32[1024]{0:T(1024)} %param.17) | copy-start | bytes 12292
  37.3 129.4 %copy-start.17 = (s32[3]{0:T(128)S(1)}, s32[3]{0:T(128)}, u32[]{:S(2)}) copy-start(s32[3]{0:T(128)} %constant.202.clone) | copy-start | bytes 40
  37.7 14.3 %collective-permute-start.4 = (bf16[4,512,128]{2,1,0:T(8,128)(2,1)S(1)}, bf16[4,512,128]{2,1,0:T(8,128)(2,1)S(1)}, u32[]{:S(2)}, u32[]{:S(2)}) collective-permute-start(bf16[4,512,128]{2,1,0:T(8,128)(2,1)S(1)} %get-tuple-element.31), channel_id=1, source_target_pairs={{0,17},{1,16},{8,25},{9,24},{16,1},{17,0},{24,9},{25,8},{2,19},{3,... | collective-permute-start | bytes 1572872 | tf_op jit(solution)/shard_map/ppermute | solution.py:28
  40.2 23.6 %collective-permute-start.3 = (bf16[4,512,128]{2,1,0:T(8,128)(2,1)S(1)}, bf16[4,512,128]{2,1,0:T(8,128)(2,1)S(1)}, u32[]{:S(2)}, u32[]{:S(2)}) collective-permute-start(bf16[4,512,128]{2,1,0:T(8,128)(2,1)S(1)} %get-tuple-element.32), channel_id=1, source_target_pairs={{0,1},{1,0},{8,9},{9,8},{16,17},{17,16},{24,25},{25,24},{2,3},{3,2... | collective-permute-start | bytes 1572872 | tf_op jit(solution)/shard_map/ppermute | solution.py:28
  40.4 23.4 %collective-permute-start.2 = (bf16[4,512,128]{2,1,0:T(8,128)(2,1)S(1)}, bf16[4,512,128]{2,1,0:T(8,128)(2,1)S(1)}, u32[]{:S(2)}, u32[]{:S(2)}) collective-permute-start(bf16[4,512,128]{2,1,0:T(8,128)(2,1)S(1)} %get-tuple-element.33), channel_id=1, source_target_pairs={{0,16},{1,17},{8,24},{9,25},{16,0},{17,1},{24,8},{25,9},{2,18},{3,... | collective-permute-start | bytes 1572872 | tf_op jit(solution)/shard_map/ppermute | solution.py:28
  64.0 55.9 %copy-start.5 = (bf16[4,2048,128]{2,1,0:T(8,128)(2,1)}, bf16[4,2048,128]{2,1,0:T(8,128)(2,1)S(1)}, u32[]{:S(2)}) copy-start(bf16[4,2048,128]{2,1,0:T(8,128)(2,1)S(1)} %pad_maximum_fusion.5) | copy-start | bytes 6291460
  64.0 47.8 %collective-permute-start.5 = (bf16[4,2048,128]{2,1,0:T(8,128)(2,1)S(1)}, bf16[4,2048,128]{2,1,0:T(8,128)(2,1)}, u32[]{:S(2)}, u32[]{:S(2)}) collective-permute-start(bf16[4,2048,128]{2,1,0:T(8,128)(2,1)S(1)} %pad_maximum_fusion.5), channel_id=1, source_target_pairs={{0,2},{2,4},{4,6},{1,3},{3,5},{5,7},{8,10},{10,12},{12,14},{9,11},... | collective-permute-start | bytes 6291464 | tf_op jit(solution)/shard_map/ppermute | solution.py:39
  68.7 48.6 %collective-permute-start.8 = (bf16[4,2048,128]{2,1,0:T(8,128)(2,1)S(1)}, bf16[4,2048,128]{2,1,0:T(8,128)(2,1)}, u32[]{:S(2)}, u32[]{:S(2)}) collective-permute-start(bf16[4,2048,128]{2,1,0:T(8,128)(2,1)S(1)} %pad_maximum_fusion.5), channel_id=1, source_target_pairs={{2,0},{4,2},{6,4},{3,1},{5,3},{7,5},{10,8},{12,10},{14,12},{11,9},... | collective-permute-start | bytes 6291464 | tf_op jit(solution)/shard_map/ppermute | solution.py:39
  111.7 48.0 %collective-permute-start.6 = (bf16[4,2048,128]{2,1,0:T(8,128)(2,1)}, bf16[4,2048,128]{2,1,0:T(8,128)(2,1)}, u32[]{:S(2)}, u32[]{:S(2)}) collective-permute-start(bf16[4,2048,128]{2,1,0:T(8,128)(2,1)} %collective-permute-done.5), channel_id=1, source_target_pairs={{0,2},{2,4},{4,6},{1,3},{3,5},{5,7},{8,10},{10,12},{12,14},{9,11},... | collective-permute-start | bytes 6291464 | tf_op jit(solution)/shard_map/ppermute | solution.py:39
  117.3 47.8 %collective-permute-start.9 = (bf16[4,2048,128]{2,1,0:T(8,128)(2,1)}, bf16[4,2048,128]{2,1,0:T(8,128)(2,1)}, u32[]{:S(2)}, u32[]{:S(2)}) collective-permute-start(bf16[4,2048,128]{2,1,0:T(8,128)(2,1)} %collective-permute-done.8), channel_id=1, source_target_pairs={{2,0},{4,2},{6,4},{3,1},{5,3},{7,5},{10,8},{12,10},{14,12},{11,9},... | collective-permute-start | bytes 6291464 | tf_op jit(solution)/shard_map/ppermute | solution.py:39
  118.6 52.1 %collective-permute-start.12 = (bf16[4,512,512]{2,1,0:T(8,128)(2,1)S(1)}, bf16[4,512,512]{2,1,0:T(8,128)(2,1)}, u32[]{:S(2)}, u32[]{:S(2)}) collective-permute-start(bf16[4,512,512]{2,1,0:T(8,128)(2,1)S(1)} %fusion.39), channel_id=1, source_target_pairs={{0,16},{1,17},{8,24},{9,25},{16,0},{17,1},{24,8},{25,9},{2,18},{3,... | collective-permute-start | bytes 6291464 | tf_op jit(solution)/shard_map/ppermute | solution.py:28
  119.9 56.2 %collective-permute-start.13 = (bf16[4,512,512]{2,1,0:T(8,128)(2,1)S(1)}, bf16[4,512,512]{2,1,0:T(8,128)(2,1)}, u32[]{:S(2)}, u32[]{:S(2)}) collective-permute-start(bf16[4,512,512]{2,1,0:T(8,128)(2,1)S(1)} %fusion.39), channel_id=1, source_target_pairs={{0,1},{1,0},{8,9},{9,8},{16,17},{17,16},{24,25},{25,24},{2,3},{3,2... | collective-permute-start | bytes 6291464 | tf_op jit(solution)/shard_map/ppermute | solution.py:28
  120.1 90.2 %collective-permute-start.14 = (bf16[4,512,512]{2,1,0:T(8,128)(2,1)S(1)}, bf16[4,512,512]{2,1,0:T(8,128)(2,1)}, u32[]{:S(2)}, u32[]{:S(2)}) collective-permute-start(bf16[4,512,512]{2,1,0:T(8,128)(2,1)S(1)} %fusion.39), channel_id=1, source_target_pairs={{0,17},{1,16},{8,25},{9,24},{16,1},{17,0},{24,9},{25,8},{2,19},{3,... | collective-permute-start | bytes 6291464 | tf_op jit(solution)/shard_map/ppermute | solution.py:28
  159.7 52.4 %collective-permute-start.7 = (bf16[4,2048,128]{2,1,0:T(8,128)(2,1)}, bf16[4,2048,128]{2,1,0:T(8,128)(2,1)}, u32[]{:S(2)}, u32[]{:S(2)}) collective-permute-start(bf16[4,2048,128]{2,1,0:T(8,128)(2,1)} %collective-permute-done.6), channel_id=1, source_target_pairs={{0,2},{2,4},{4,6},{1,3},{3,5},{5,7},{8,10},{10,12},{12,14},{9,11},... | collective-permute-start | bytes 6291464 | tf_op jit(solution)/shard_map/ppermute | solution.py:39
  165.2 50.2 %collective-permute-start.10 = (bf16[4,2048,128]{2,1,0:T(8,128)(2,1)}, bf16[4,2048,128]{2,1,0:T(8,128)(2,1)}, u32[]{:S(2)}, u32[]{:S(2)}) collective-permute-start(bf16[4,2048,128]{2,1,0:T(8,128)(2,1)} %collective-permute-done.9), channel_id=1, source_target_pairs={{2,0},{4,2},{6,4},{3,1},{5,3},{7,5},{10,8},{12,10},{14,12},{11,9},... | collective-permute-start | bytes 6291464 | tf_op jit(solution)/shard_map/ppermute | solution.py:39
  170.7 55.3 %collective-permute-start.15 = (bf16[4,2048,128]{2,1,0:T(8,128)(2,1)}, bf16[4,2048,128]{2,1,0:T(8,128)(2,1)}, u32[]{:S(2)}, u32[]{:S(2)}) collective-permute-start(bf16[4,2048,128]{2,1,0:T(8,128)(2,1)} %copy-done.5), channel_id=1, source_target_pairs={{0,8},{8,0},{16,24},{24,16},{1,9},{9,1},{17,25},{25,17},{2,10},{10... | collective-permute-start | bytes 6291464 | tf_op jit(solution)/shard_map/ppermute | solution.py:32
  212.1 3.3 copy-start.7
  221.6 32.6 %collective-permute-start.16 = (bf16[4,2048,128]{2,1,0:T(8,128)(2,1)}, bf16[4,2048,128]{2,1,0:T(8,128)(2,1)}, u32[]{:S(2)}, u32[]{:S(2)}) collective-permute-start(bf16[4,2048,128]{2,1,0:T(8,128)(2,1)} %get-tuple-element.23), channel_id=1, source_target_pairs={{0,8},{8,0},{16,24},{24,16},{1,9},{9,1},{17,25},{25,17},{2,10},{10... | collective-permute-start | bytes 6291464 | tf_op jit(solution)/shard_map/ppermute | solution.py:32
  253.7 43.5 %collective-permute-start.17 = (bf16[4,2048,128]{2,1,0:T(8,128)(2,1)S(1)}, bf16[4,2048,128]{2,1,0:T(8,128)(2,1)}, u32[]{:S(2)}, u32[]{:S(2)}) collective-permute-start(bf16[4,2048,128]{2,1,0:T(8,128)(2,1)S(1)} %get-tuple-element.22), channel_id=1, source_target_pairs={{0,8},{8,0},{16,24},{24,16},{1,9},{9,1},{17,25},{25,17},{2,10},{10... | collective-permute-start | bytes 6291464 | tf_op jit(solution)/shard_map/ppermute | solution.py:32
  253.7 4.6 copy-start.8
  253.7 89.6 %collective-permute-start.11 = (bf16[4,2048,128]{2,1,0:T(8,128)(2,1)}, bf16[4,2048,128]{2,1,0:T(8,128)(2,1)}, u32[]{:S(2)}, u32[]{:S(2)}) collective-permute-start(bf16[4,2048,128]{2,1,0:T(8,128)(2,1)} %get-tuple-element.21), channel_id=1, source_target_pairs={{0,8},{8,0},{16,24},{24,16},{1,9},{9,1},{17,25},{25,17},{2,10},{10... | collective-permute-start | bytes 6291464 | tf_op jit(solution)/shard_map/ppermute | solution.py:32
  299.2 15.0 %copy-start = (bf16[4,2048,256]{2,1,0:T(8,128)(2,1)}, bf16[4,2048,256]{2,1,0:T(8,128)(2,1)S(1)}, u32[]{:S(2)}) copy-start(bf16[4,2048,256]{2,1,0:T(8,128)(2,1)S(1)} %pad_maximum_fusion.3) | copy-start | bytes 12582916
  330.4 13.0 %copy-start.4 = (bf16[4,2048,128]{2,1,0:T(8,128)(2,1)S(1)}, bf16[4,2048,128]{2,1,0:T(8,128)(2,1)}, u32[]{:S(2)}) copy-start(bf16[4,2048,128]{2,1,0:T(8,128)(2,1)} %get-tuple-element.21) | copy-start | bytes 6291460
  330.4 13.0 %copy-start.15 = (f32[512,4]{0,1:T(4,128)S(1)}, f32[512,4]{0,1:T(4,128)}, u32[]{:S(2)}) copy-start(f32[512,4]{0,1:T(4,128)} %get-tuple-element.49) | copy-start | bytes 24580
  343.4 13.7 %copy-start.14 = (f32[512,4]{0,1:T(4,128)S(1)}, f32[512,4]{0,1:T(4,128)}, u32[]{:S(2)}) copy-start(f32[512,4]{0,1:T(4,128)} %get-tuple-element.48) | copy-start | bytes 24580
  356.8 48.0 %collective-permute-start.27 = (bf16[2,512,512]{2,1,0:T(8,128)(2,1)}, bf16[2,512,512]{2,1,0:T(8,128)(2,1)S(1)}, u32[]{:S(2)}, u32[]{:S(2)}) collective-permute-start(bf16[2,512,512]{2,1,0:T(8,128)(2,1)} %bitcast.50), channel_id=1, source_target_pairs={{0,1},{1,0},{8,9},{9,8},{16,17},{17,16},{24,25},{25,24},{2,3},{3,2... | collective-permute-start | bytes 3145736 | tf_op jit(solution)/shard_map/ppermute | solution.py:28
  357.1 15.8 %copy-start.13 = (f32[512,4]{0,1:T(4,128)S(1)}, f32[512,4]{0,1:T(4,128)}, u32[]{:S(2)}) copy-start(f32[512,4]{0,1:T(4,128)} %get-tuple-element.47) | copy-start | bytes 24580
  371.6 36.0 %collective-permute-start.24 = (bf16[2,512,512]{2,1,0:T(8,128)(2,1)}, bf16[2,512,512]{2,1,0:T(8,128)(2,1)S(1)}, u32[]{:S(2)}, u32[]{:S(2)}) collective-permute-start(bf16[2,512,512]{2,1,0:T(8,128)(2,1)} %bitcast.42), channel_id=1, source_target_pairs={{0,1},{1,0},{8,9},{9,8},{16,17},{17,16},{24,25},{25,24},{2,3},{3,2... | collective-permute-start | bytes 3145736 | tf_op jit(solution)/shard_map/ppermute | solution.py:28
  372.8 15.2 %copy-start.12 = (f32[512,4]{0,1:T(4,128)S(1)}, f32[512,4]{0,1:T(4,128)}, u32[]{:S(2)}) copy-start(f32[512,4]{0,1:T(4,128)} %get-tuple-element.46) | copy-start | bytes 24580
  387.8 38.4 %collective-permute-start.21 = (bf16[2,512,512]{2,1,0:T(8,128)(2,1)}, bf16[2,512,512]{2,1,0:T(8,128)(2,1)S(1)}, u32[]{:S(2)}, u32[]{:S(2)}) collective-permute-start(bf16[2,512,512]{2,1,0:T(8,128)(2,1)} %bitcast.34), channel_id=1, source_target_pairs={{0,1},{1,0},{8,9},{9,8},{16,17},{17,16},{24,25},{25,24},{2,3},{3,2... | collective-permute-start | bytes 3145736 | tf_op jit(solution)/shard_map/ppermute | solution.py:28
  403.5 45.2 %collective-permute-start.18 = (bf16[2,512,512]{2,1,0:T(8,128)(2,1)S(1)}, bf16[2,512,512]{2,1,0:T(8,128)(2,1)S(1)}, u32[]{:S(2)}, u32[]{:S(2)}) collective-permute-start(bf16[2,512,512]{2,1,0:T(8,128)(2,1)S(1)} %bitcast.143), channel_id=1, source_target_pairs={{0,1},{1,0},{8,9},{9,8},{16,17},{17,16},{24,25},{25,24},{2,3},{3,2... | collective-permute-start | bytes 3145736 | tf_op jit(solution)/shard_map/ppermute | solution.py:28
  405.2 44.2 %collective-permute-start.28 = (bf16[2,512,512]{2,1,0:T(8,128)(2,1)S(1)}, bf16[2,512,512]{2,1,0:T(8,128)(2,1)S(1)}, u32[]{:S(2)}, u32[]{:S(2)}) collective-permute-start(bf16[2,512,512]{2,1,0:T(8,128)(2,1)S(1)} %fusion.45), channel_id=1, source_target_pairs={{0,16},{1,17},{8,24},{9,25},{16,0},{17,1},{24,8},{25,9},{2,18},{3,... | collective-permute-start | bytes 3145736 | tf_op jit(solution)/shard_map/ppermute | solution.py:28
  408.0 44.5 %collective-permute-start.25 = (bf16[2,512,512]{2,1,0:T(8,128)(2,1)S(1)}, bf16[2,512,512]{2,1,0:T(8,128)(2,1)S(1)}, u32[]{:S(2)}, u32[]{:S(2)}) collective-permute-start(bf16[2,512,512]{2,1,0:T(8,128)(2,1)S(1)} %fusion.44), channel_id=1, source_target_pairs={{0,16},{1,17},{8,24},{9,25},{16,0},{17,1},{24,8},{25,9},{2,18},{3,... | collective-permute-start | bytes 3145736 | tf_op jit(solution)/shard_map/ppermute | solution.py:28
  426.6 46.7 %collective-permute-start.22 = (bf16[2,512,512]{2,1,0:T(8,128)(2,1)S(1)}, bf16[2,512,512]{2,1,0:T(8,128)(2,1)S(1)}, u32[]{:S(2)}, u32[]{:S(2)}) collective-permute-start(bf16[2,512,512]{2,1,0:T(8,128)(2,1)S(1)} %fusion.43), channel_id=1, source_target_pairs={{0,16},{1,17},{8,24},{9,25},{16,0},{17,1},{24,8},{25,9},{2,18},{3,... | collective-permute-start | bytes 3145736 | tf_op jit(solution)/shard_map/ppermute | solution.py:28
  449.1 46.7 %collective-permute-start.19 = (bf16[2,512,512]{2,1,0:T(8,128)(2,1)S(1)}, bf16[2,512,512]{2,1,0:T(8,128)(2,1)S(1)}, u32[]{:S(2)}, u32[]{:S(2)}) collective-permute-start(bf16[2,512,512]{2,1,0:T(8,128)(2,1)S(1)} %fusion.42), channel_id=1, source_target_pairs={{0,16},{1,17},{8,24},{9,25},{16,0},{17,1},{24,8},{25,9},{2,18},{3,... | collective-permute-start | bytes 3145736 | tf_op jit(solution)/shard_map/ppermute | solution.py:28
  450.9 48.0 %collective-permute-start.29 = (bf16[2,512,512]{2,1,0:T(8,128)(2,1)}, bf16[2,512,512]{2,1,0:T(8,128)(2,1)}, u32[]{:S(2)}, u32[]{:S(2)}) collective-permute-start(bf16[2,512,512]{2,1,0:T(8,128)(2,1)} %add_convert_fusion), channel_id=1, source_target_pairs={{0,8},{8,0},{16,24},{24,16},{1,9},{9,1},{17,25},{25,17},{2,10},{10... | collective-permute-start | bytes 3145736 | tf_op jit(solution)/shard_map/ppermute | solution.py:32
  453.0 47.6 %collective-permute-start.26 = (bf16[2,512,512]{2,1,0:T(8,128)(2,1)S(1)}, bf16[2,512,512]{2,1,0:T(8,128)(2,1)}, u32[]{:S(2)}, u32[]{:S(2)}) collective-permute-start(bf16[2,512,512]{2,1,0:T(8,128)(2,1)S(1)} %add_convert_fusion.1), channel_id=1, source_target_pairs={{0,8},{8,0},{16,24},{24,16},{1,9},{9,1},{17,25},{25,17},{2,10},{10... | collective-permute-start | bytes 3145736 | tf_op jit(solution)/shard_map/ppermute | solution.py:32
  473.8 28.3 %collective-permute-start.23 = (bf16[2,512,512]{2,1,0:T(8,128)(2,1)S(1)}, bf16[2,512,512]{2,1,0:T(8,128)(2,1)}, u32[]{:S(2)}, u32[]{:S(2)}) collective-permute-start(bf16[2,512,512]{2,1,0:T(8,128)(2,1)S(1)} %add_convert_fusion.2), channel_id=1, source_target_pairs={{0,8},{8,0},{16,24},{24,16},{1,9},{9,1},{17,25},{25,17},{2,10},{10... | collective-permute-start | bytes 3145736 | tf_op jit(solution)/shard_map/ppermute | solution.py:32
  496.3 7.3 %collective-permute-start.20 = (bf16[2,512,512]{2,1,0:T(8,128)(2,1)S(1)}, bf16[2,512,512]{2,1,0:T(8,128)(2,1)}, u32[]{:S(2)}, u32[]{:S(2)}) collective-permute-start(bf16[2,512,512]{2,1,0:T(8,128)(2,1)S(1)} %add_convert_fusion.3), channel_id=1, source_target_pairs={{0,8},{8,0},{16,24},{24,16},{1,9},{9,1},{17,25},{25,17},{2,10},{10... | collective-permute-start | bytes 3145736 | tf_op jit(solution)/shard_map/ppermute | solution.py:32
  506.2 3.4 copy-start.9
  506.2 3.4 copy-start.10
  (4 other events, 8.3 us)

commit v2 on v1

--- a/solution.py
+++ b/solution.py
@@ -62,14 +62,25 @@
     keys = [plane_shift(key_columns(s, t), s, t) if s or t else key_columns(0, 0) for t, s in turns]
     own_keys = jnp.concatenate(keys, 1)
     transformed, own_keys = lax.optimization_barrier((transformed, own_keys))
-    queries = jnp.concatenate(
-        [plane_shift(transformed, s, t) if s or t else transformed for t, s in turns], 1
-    )
+    near = {(t, s): plane_shift(transformed, s, t) for t, s in turns if (s == 0) != (t == 0)}
+    far_turns = [(t, s) for t, s in turns if s and t]
+    far = {}
 
     up, down = [own_keys], [own_keys]
-    for _ in range(blk_size - 1):
-        up.append(line(up[-1], 1))
-        down.append(line(down[-1], -1))
+    for step in range(1, blk_size):
+        before = (up[-1], down[-1])
+        if step == 2:
+            before, near = lax.optimization_barrier((before, near))
+        if step == 3:
+            before, far = lax.optimization_barrier((before, far))
+        up.append(line(before[0], 1))
+        down.append(line(before[1], -1))
+        if step == 2:
+            far = {(t, s): plane_shift(transformed, s, t) for t, s in far_turns}
+    if blk_size < 3:
+        far = {(t, s): plane_shift(transformed, s, t) for t, s in far_turns}
+    held = {(0, 0): transformed, **near, **far}
+    queries = jnp.concatenate([held[turn] for turn in turns], 1)
 
     def arrival(z, stage):
         others = sorted((b for b in range(blk_size)), key=lambda b: (abs(b - z), b))
@@ -102,7 +113,7 @@
         energy = lax.dynamic_slice_in_dim(occ_energy, source * occ_block, occ_block)
         return gathered_cores(chosen, 2), energy
 
-    def pair_step(rows, energy_rows, visiting, visit_energy):
+    def amplitudes(rows, energy_rows, visiting, visit_energy):
         tiles = jnp.einsum("ipa,jpb->iajb", rows, visiting, preferred_element_type=jnp.float32)
         denominator = (
             energy_rows[:, None, None, None]
@@ -110,32 +121,39 @@
             - own_virtual[None, :, None, None]
             - key_virtual[None, None, None, :]
         )
-        amplitude = (1.3 * tiles / denominator).astype(jnp.bfloat16)
-        return jnp.einsum("iajb,jpb->ipa", amplitude, visiting, preferred_element_type=jnp.float32)
+        return (1.3 * tiles / denominator).astype(jnp.bfloat16)
 
-    totals = None
-    for stage in range(blk_size - 1):
-        visiting, visit_energy = stage_keys(stage)
-        if totals is not None:
-            totals, visiting = lax.optimization_barrier((totals, visiting))
-        term = pair_step(queries, own_energy, visiting, visit_energy)
-        totals = term if totals is None else totals + term
+    def contracted(amplitude, visiting):
+        return jnp.einsum("ajb,jpb->pa", amplitude, visiting, preferred_element_type=jnp.float32)
+
+    early = [stage_keys(stage) for stage in range(blk_size - 1)]
+    early_amplitude = None
+    if early:
+        early_keys = jnp.concatenate([k for k, _ in early], 0)
+        early_energy = jnp.concatenate([e for _, e in early], 0)
+        early_amplitude = amplitudes(queries, own_energy, early_keys, early_energy)
     visiting, visit_energy = stage_keys(blk_size - 1)
-    wide = []
+    parts, wide = [], []
     for i in range(occ_block):
-        part = pair_step(queries[i : i + 1], own_energy[i : i + 1], visiting, visit_energy)[0]
-        if totals is not None:
-            part = part + totals[i]
+        rows, before = queries[i : i + 1], None if early_amplitude is None else early_amplitude[i]
+        if parts:
+            rows, before, parts[-1] = lax.optimization_barrier((rows, before, parts[-1]))
+        part = contracted(amplitudes(rows, own_energy[i : i + 1], visiting, visit_energy)[0], visiting)
+        if before is not None:
+            part = part + contracted(before, early_keys)
         part = part.reshape(aux_size, xs, quarter, vir_part)
-        half = part[0]
-        for t in range(1, aux_size):
-            half = half + plane_shift(part[(-t) % aux_size].astype(jnp.bfloat16), 0, t)
+        away = [plane_shift(part[(-t) % aux_size].astype(jnp.bfloat16), 0, t) for t in range(1, aux_size)]
+        parts.append(part[0])
+        wide.append(away)
+    for i in range(occ_block):
+        half = parts[i]
+        for received in wide[i]:
+            half = half + received
         total = half
         for s in range(1, xs):
             received = plane_shift(half.astype(jnp.bfloat16), s, 0)
             total = total + jnp.roll(received, s, 0)
-        whole = gathered_cores(total.astype(jnp.bfloat16), 2)
-        wide.append(whole)
+        wide[i] = gathered_cores(total.astype(jnp.bfloat16), 2)
     wide = jnp.stack(wide)
     wide = jnp.concatenate(
         [lax.dynamic_slice_in_dim(wide, (x_index - p) % xs, 1, 1)[:, 0] for p in range(xs)], 1

time: 526 us -> 503 us (0.956)
  other arithmetic: 52.6 us -> 31.5 us
  matrix products: 142 us -> 128 us
  waiting for transfers between devices: 228 us -> 237 us
    ppermute x15, waiting for transfers between devices: 152 us -> 194 us  [plane_shift(): return lax.ppermute(v, ('sec', 'aux'), perm)]
    ppermute x6, waiting for transfers between devices: 75.6 us -> 42.3 us  [line(): return lax.ppermute(v, 'blk', perm)]
    add x5 -> x3, other arithmetic: 27.6 us -> 2.61 us  [amplitudes(): energy_rows[:, None, None, None] + visit_energy[None, None, :, None]]
    dot_general x9, matrix products: 133 us -> 120 us  [the longest x8 85.8 us: contracted(): jnp.einsum('ajb,jpb->pa', amplitude, visiting, preferred_element_type=jnp...]
    squeeze x0 -> x1, local copies, waits for them, and re-layouts: none -> 5.95 us  [shards(): early_amplitude[i]]
    unnamed x47 -> x65, local copies, waits for them, and re-layouts: 11.6 us -> 10.6 us
    slice x8 -> x9, local copies, waits for them, and re-layouts: 10.7 us -> 10.4 us  [the longest x4 4.13 us: shards(): part[-t % aux_size].astype(jnp.bfloat16)]
  transfers between devices with their start and end apart: 30 -> 30, of which waited for: 11 -> 17; matrix products, arithmetic and copies ran while one was open for 37% -> 25% of each run, Pallas kernels for 0% -> 0%
where the time goes in v2:
time: 503 us; the launch traced here: 498 us
  waiting for transfers between devices  237 us (47%)
  matrix products  128 us (25%)
  starting transfers between devices  54.3 us (11%)
  local copies, waits for them, and re-layouts  43.5 us (9%)
  other arithmetic  31.5 us (6%)
    ppermute x15, waiting for transfers between devices, plane_shift(): return lax.ppermute(v, ('sec', 'aux'), perm)  194 us
    dot_general x8, matrix products, contracted(): jnp.einsum('ajb,jpb->pa', amplitude, visiting, preferred_element_type=jnp...  85.8 us
    ppermute x6, waiting for transfers between devices, line(): return lax.ppermute(v, 'blk', perm)  42.3 us
    dot_general x1, matrix products, amplitudes(): jnp.einsum('ipa,jpb->iajb', rows, visiting, preferred_element_type=jnp.fl...  34.3 us
    ppermute x9, starting transfers between devices, core_shift(): return lax.ppermute(v, 'sec', perm)  20 us
    ppermute x15, starting transfers between devices, plane_shift(): return lax.ppermute(v, ('sec', 'aux'), perm)  17.5 us
    ppermute x6, starting transfers between devices, line(): return lax.ppermute(v, 'blk', perm)  16.8 us
    unnamed x65, local copies, waits for them, and re-layouts  10.6 us
  transfers between devices with their start and end apart: 30, of which 17 were waited for; matrix products, arithmetic and copies ran while one was open for 25% of the time, Pallas kernels for 0%

profile of v2, /device:TPU:1, one launch (start us, length us, event | category | flops | bytes accessed | tf_op | source)
XLA Modules:
  0.0 497.7 jit_solution(14889936215330512052)
XLA Ops:
  1.7 2.1 collective-permute-start
  3.8 22.9 %collective-permute-done = bf16[4,512,256]{2,1,0:T(8,128)(2,1)S(1)} collective-permute-done((bf16[4,512,256]{2,1,0:T(8,128)(2,1)S(1)}, bf16[4,512,256]{2,1,0:T(8,128)(2,1)S(1)}, u32[]{:S(2)}, u32[]{:S(2)}) %collective-permute-start) | collective-permute-done | bytes 1048608 | tf_op jit(solution)/shard_map/ppermute | solution.py:28
  29.1 3.4 fusion.60
  33.0 3.9 fusion.22
  37.5 2.5 collective-permute-start.4
  40.3 11.4 %collective-permute-done.4 = bf16[4,512,128]{2,1,0:T(8,128)(2,1)S(1)} collective-permute-done((bf16[4,512,128]{2,1,0:T(8,128)(2,1)S(1)}, bf16[4,512,128]{2,1,0:T(8,128)(2,1)S(1)}, u32[]{:S(2)}, u32[]{:S(2)}) %collective-permute-start.4) | collective-permute-done | bytes 524320 | tf_op jit(solution)/shard_map/ppermute | solution.py:28
  51.7 11.8 %collective-permute-done.3 = bf16[4,512,128]{2,1,0:T(8,128)(2,1)S(1)} collective-permute-done((bf16[4,512,128]{2,1,0:T(8,128)(2,1)S(1)}, bf16[4,512,128]{2,1,0:T(8,128)(2,1)S(1)}, u32[]{:S(2)}, u32[]{:S(2)}) %collective-permute-start.3) | collective-permute-done | bytes 524320 | tf_op jit(solution)/shard_map/ppermute | solution.py:28
  66.6 4.1 collective-permute-start.5
  72.0 38.2 %collective-permute-done.8 = bf16[4,512,512]{2,1,0:T(8,128)(2,1)S(1)} collective-permute-done((bf16[4,512,512]{2,1,0:T(8,128)(2,1)S(1)}, bf16[4,512,512]{2,1,0:T(8,128)(2,1)S(1)}, u32[]{:S(2)}, u32[]{:S(2)}) %collective-permute-start.8) | collective-permute-done | bytes 2097184 | tf_op jit(solution)/shard_map/ppermute | solution.py:28
  113.8 5.5 %collective-permute-start.9 = (bf16[4,2048,128]{2,1,0:T(8,128)(2,1)S(1)}, bf16[4,2048,128]{2,1,0:T(8,128)(2,1)}, u32[]{:S(2)}, u32[]{:S(2)}) collective-permute-start(bf16[4,2048,128]{2,1,0:T(8,128)(2,1)S(1)} %collective-permute-done.5), channel_id=1, source_target_pairs={{0,2},{2,4},{4,6},{1,3},{3,5},{5,7},{8,10},{10,12},{12,14},{9,11},... | collective-permute-start | bytes 6291464 | tf_op jit(solution)/shard_map/ppermute | solution.py:39
  120.6 35.5 %collective-permute-done.11 = bf16[4,512,512]{2,1,0:T(8,128)(2,1)S(1)} collective-permute-done((bf16[4,512,512]{2,1,0:T(8,128)(2,1)S(1)}, bf16[4,512,512]{2,1,0:T(8,128)(2,1)S(1)}, u32[]{:S(2)}, u32[]{:S(2)}) %collective-permute-start.11) | collective-permute-done | bytes 2097184 | tf_op jit(solution)/shard_map/ppermute | solution.py:28
  156.1 4.1 collective-permute-done.9
  160.2 5.3 %collective-permute-done.10 = bf16[4,2048,128]{2,1,0:T(8,128)(2,1)} collective-permute-done((bf16[4,2048,128]{2,1,0:T(8,128)(2,1)S(1)}, bf16[4,2048,128]{2,1,0:T(8,128)(2,1)}, u32[]{:S(2)}, u32[]{:S(2)}) %collective-permute-start.10) | collective-permute-done | bytes 2097184 | tf_op jit(solution)/shard_map/ppermute | solution.py:39
  165.5 2.9 collective-permute-start.15
  168.4 1.7 collective-permute-start.16
  176.7 1.8 broadcast_add_fusion.2
  178.5 4.3 collective-permute-start.12
  182.8 25.6 %collective-permute-done.15 = bf16[4,2048,128]{2,1,0:T(8,128)(2,1)} collective-permute-done((bf16[4,2048,128]{2,1,0:T(8,128)(2,1)}, bf16[4,2048,128]{2,1,0:T(8,128)(2,1)}, u32[]{:S(2)}, u32[]{:S(2)}) %collective-permute-start.15) | collective-permute-done | bytes 2097184 | tf_op jit(solution)/shard_map/ppermute | solution.py:39
  208.4 5.1 %collective-permute-done.16 = bf16[4,2048,128]{2,1,0:T(8,128)(2,1)} collective-permute-done((bf16[4,2048,128]{2,1,0:T(8,128)(2,1)}, bf16[4,2048,128]{2,1,0:T(8,128)(2,1)}, u32[]{:S(2)}, u32[]{:S(2)}) %collective-permute-start.16) | collective-permute-done | bytes 2097184 | tf_op jit(solution)/shard_map/ppermute | solution.py:39
  213.5 5.0 select_select_fusion
  218.5 5.2 %collective-permute-start.14 = (bf16[4,2048,128]{2,1,0:T(8,128)(2,1)S(1)}, bf16[4,2048,128]{2,1,0:T(8,128)(2,1)S(1)}, u32[]{:S(2)}, u32[]{:S(2)}) collective-permute-start(bf16[4,2048,128]{2,1,0:T(8,128)(2,1)S(1)} %get-tuple-element.52), channel_id=1, source_target_pairs={{0,8},{8,0},{16,24},{24,16},{1,9},{9,1},{17,25},{25,17},{2,10},{10... | collective-permute-start | bytes 6291464 | tf_op jit(solution)/shard_map/ppermute | solution.py:32
  228.2 2.9 fusion.59
  231.1 2.4 copy-done.3
  234.6 5.2 %maximum_maximum_fusion = bf16[12,2048,256]{2,1,0:T(8,128)(2,1)S(1)} fusion(bf16[4,2048,128]{2,1,0:T(8,128)(2,1)S(1)} %collective-permute-done.14, bf16[4,2048,128]{2,1,0:T(8,128)(2,1)S(1)} %get-tuple-element.52, bf16[4,2048,128]{2,1,0:T(8,128)(2,1)} %collective-permute-done.13, bf16[4,2048,128]{2,1,0:T(8,128)(2,1)S(1)} %get-tuple-element.53, ...), kind=kLoop, calls=%fused_computation.1 | loop fusion | flops 75497472 | bytes 25165824 | tf_op jit(solution)/shard_map/concatenate | solution.py:132
  239.9 34.3 %divide_convert_fusion = bf16[4,512,12,256]{3,1,2,0:T(8,128)(2,1)} fusion(bf16[12,2048,256]{2,1,0:T(8,128)(2,1)S(1)} %maximum_maximum_fusion, f32[256]{0:T(256)S(1)} %pad_maximum_fusion.4, f32[4,512,12]{1,2,0:T(8,128)S(1)} %broadcast_subtract_fusion, bf16[4,2048,512]{2,1,0:T(8,128)(2,1)} %copy-done.3), kind=kOutput, calls=%fused_computation | convolution fusion | flops 25794969600 | bytes 33653760 | tf_op jit(solution)/shard_map/ipa,jpb->iajb/dot_general | solution.py:117
  274.2 5.9 %slice_bitcast_fusion.4 = (bf16[512,12,256]{2,0,1:T(8,128)(2,1)S(1)}, bf16[512,12,256]{2,0,1:T(8,128)(2,1)}, bf16[512,12,256]{2,0,1:T(8,128)(2,1)}) fusion(bf16[4,512,12,256]{3,1,2,0:T(8,128)(2,1)} %divide_convert_fusion), kind=kLoop, calls=%fused_computation.26 | loop fusion | bytes 18874368 | tf_op jit(solution)/shard_map/squeeze | solution.py:138
  281.5 10.6 %fusion.41 = f32[2048,512,1]{1,0,2:T(8,128)} fusion(bf16[4,2048,512]{2,1,0:T(8,128)(2,1)} %copy-done.3, f32[256]{0:T(256)S(1)} %pad_maximum_fusion.4, f32[512,4]{0,1:T(4,128)S(1)} %get-tuple-element.79, bf16[4,2048,128]{2,1,0:T(8,128)(2,1)} %copy-done.25, bf16[4,2048,128]{2,1,0:T(8,128)(2,1)} %copy-done.9), kind=kOutput, calls=%fused_computation.72 | convolution fusion | flops 4313841664 | bytes 14689280 | tf_op jit(solution)/shard_map/ajb,jpb->pa/dot_general | solution.py:127
  292.1 11.2 %bitcast_add_fusion.3 = f32[2048,512]{1,0:T(8,128)S(1)} fusion(f32[2048,512,1]{1,0,2:T(8,128)} %fusion.41, bf16[12,2048,256]{2,1,0:T(8,128)(2,1)} %copy-done.2, bf16[4,512,12,256]{3,1,2,0:T(8,128)(2,1)} %divide_convert_fusion), kind=kOutput, calls=%fused_computation.20 | convolution fusion | flops 6443499520 | bytes 24117248 | tf_op jit(solution)/shard_map/ajb,jpb->pa/dot_general | solution.py:127
  306.0 10.6 %fusion.43 = f32[2048,512,1]{1,0,2:T(8,128)} fusion(bf16[1,2048,512]{2,1,0:T(8,128)(2,1)} %get-tuple-element.33, f32[512,4]{0,1:T(4,128)S(1)} %get-tuple-element.77, f32[256]{0:T(256)S(1)} %pad_maximum_fusion.4, bf16[4,2048,128]{2,1,0:T(8,128)(2,1)} %copy-done.25, bf16[4,2048,128]{2,1,0:T(8,128)(2,1)} %copy-done.9), kind=kOutput, calls=%fused_computation.73 | convolution fusion | flops 4313841664 | bytes 10494976 | tf_op jit(solution)/shard_map/ajb,jpb->pa/dot_general | solution.py:127
  316.6 10.5 %bitcast_add_fusion.2 = f32[2048,512]{1,0:T(8,128)S(1)} fusion(f32[2048,512,1]{1,0,2:T(8,128)} %fusion.43, bf16[12,2048,256]{2,1,0:T(8,128)(2,1)} %copy-done.2, bf16[512,12,256]{2,0,1:T(8,128)(2,1)S(1)} %get-tuple-element.34), kind=kOutput, calls=%fused_computation.19 | convolution fusion | flops 6443499520 | bytes 24117248 | tf_op jit(solution)/shard_map/ajb,jpb->pa/dot_general | solution.py:127
  329.8 2.1 collective-permute-start.18
  332.0 9.4 %fusion.46 = f32[2048,512,1]{1,0,2:T(8,128)} fusion(bf16[1,2048,512]{2,1,0:T(8,128)(2,1)} %get-tuple-element.36, f32[512,4]{0,1:T(4,128)S(1)} %copy-done.23, f32[256]{0:T(256)S(1)} %pad_maximum_fusion.4, bf16[4,2048,128]{2,1,0:T(8,128)(2,1)} %copy-done.25, bf16[4,2048,128]{2,1,0:T(8,128)(2,1)S(1)} %copy-done.10), kind=kOutput, calls=%fused_computation.74 | convolution fusion | flops 4313841664 | bytes 10494976 | tf_op jit(solution)/shard_map/ajb,jpb->pa/dot_general | solution.py:127
  341.4 11.2 %bitcast_add_fusion.1 = f32[2048,512]{1,0:T(8,128)S(1)} fusion(f32[2048,512,1]{1,0,2:T(8,128)} %fusion.46, bf16[12,2048,256]{2,1,0:T(8,128)(2,1)} %copy-done.2, bf16[512,12,256]{2,0,1:T(8,128)(2,1)} %get-tuple-element.37), kind=kOutput, calls=%fused_computation.18 | convolution fusion | flops 6443499520 | bytes 24117248 | tf_op jit(solution)/shard_map/ajb,jpb->pa/dot_general | solution.py:127
  352.7 1.9 copy-done.6
  355.3 10.6 %fusion.49 = f32[2048,512,1]{1,0,2:T(8,128)} fusion(bf16[1,2048,512]{2,1,0:T(8,128)(2,1)} %get-tuple-element.39, f32[512,4]{0,1:T(4,128)S(1)} %copy-done.22, f32[256]{0:T(256)S(1)} %pad_maximum_fusion.4, bf16[4,2048,128]{2,1,0:T(8,128)(2,1)} %copy-done.25, bf16[4,2048,128]{2,1,0:T(8,128)(2,1)} %copy-done.9), kind=kOutput, calls=%fused_computation.75 | convolution fusion | flops 4313841664 | bytes 10494976 | tf_op jit(solution)/shard_map/ajb,jpb->pa/dot_general | solution.py:127
  365.9 11.5 %bitcast_add_fusion = f32[2048,512]{1,0:T(8,128)S(1)} fusion(f32[2048,512,1]{1,0,2:T(8,128)} %fusion.49, bf16[12,2048,256]{2,1,0:T(8,128)(2,1)} %copy-done.2, bf16[512,12,256]{2,0,1:T(8,128)(2,1)} %get-tuple-element.40), kind=kOutput, calls=%fused_computation.17 | convolution fusion | flops 6443499520 | bytes 24117248 | tf_op jit(solution)/shard_map/ajb,jpb->pa/dot_general | solution.py:127
  386.2 15.9 %collective-permute-done.27 = bf16[2,512,512]{2,1,0:T(8,128)(2,1)S(1)} collective-permute-done((bf16[2,512,512]{2,1,0:T(8,128)(2,1)S(1)}, bf16[2,512,512]{2,1,0:T(8,128)(2,1)S(1)}, u32[]{:S(2)}, u32[]{:S(2)}) %collective-permute-start.27) | collective-permute-done | bytes 1048608 | tf_op jit(solution)/shard_map/ppermute | solution.py:28
  403.9 20.7 %collective-permute-done.24 = bf16[2,512,512]{2,1,0:T(8,128)(2,1)S(1)} collective-permute-done((bf16[2,512,512]{2,1,0:T(8,128)(2,1)S(1)}, bf16[2,512,512]{2,1,0:T(8,128)(2,1)S(1)}, u32[]{:S(2)}, u32[]{:S(2)}) %collective-permute-start.24) | collective-permute-done | bytes 1048608 | tf_op jit(solution)/shard_map/ppermute | solution.py:28
  426.4 2.7 add_convert_fusion.3
  433.7 17.8 %collective-permute-done.28 = bf16[2,512,512]{2,1,0:T(8,128)(2,1)S(1)} collective-permute-done((bf16[2,512,512]{2,1,0:T(8,128)(2,1)S(1)}, bf16[2,512,512]{2,1,0:T(8,128)(2,1)S(1)}, u32[]{:S(2)}, u32[]{:S(2)}) %collective-permute-start.28) | collective-permute-done | bytes 1048608 | tf_op jit(solution)/shard_map/ppermute | solution.py:28
  452.0 3.2 collective-permute-start.29
  455.2 18.8 %collective-permute-done.25 = bf16[2,512,512]{2,1,0:T(8,128)(2,1)S(1)} collective-permute-done((bf16[2,512,512]{2,1,0:T(8,128)(2,1)S(1)}, bf16[2,512,512]{2,1,0:T(8,128)(2,1)S(1)}, u32[]{:S(2)}, u32[]{:S(2)}) %collective-permute-start.25) | collective-permute-done | bytes 1048608 | tf_op jit(solution)/shard_map/ppermute | solution.py:28
  475.5 1.8 collective-permute-start.26
  477.2 1.8 maximum_bitcast_fusion
  479.0 1.8 maximum_bitcast_fusion.1
  484.9 3.4 dynamic-slice_bitcast_fusion.1
  488.3 4.2 fusion.4
  492.5 4.7 copy.16
  (141 shorter events, 55.1 us)
Async XLA Ops:
  1.7 25.0 %collective-permute-start = (bf16[4,512,256]{2,1,0:T(8,128)(2,1)S(1)}, bf16[4,512,256]{2,1,0:T(8,128)(2,1)S(1)}, u32[]{:S(2)}, u32[]{:S(2)}) collective-permute-start(bf16[4,512,256]{2,1,0:T(8,128)(2,1)S(1)} %get-tuple-element.65), channel_id=1, source_target_pairs={{0,16},{1,17},{8,24},{9,25},{16,0},{17,1},{24,8},{25,9},{2,18},{3,... | collective-permute-start | bytes 3145736 | tf_op jit(solution)/shard_map/ppermute | solution.py:28
  27.8 5.2 %collective-permute-start.1 = (bf16[4,512,512]{2,1,0:T(8,128)(2,1)S(1)}, bf16[4,512,512]{2,1,0:T(8,128)(2,1)}, u32[]{:S(2)}, u32[]{:S(2)}) collective-permute-start(bf16[4,512,512]{2,1,0:T(8,128)(2,1)S(1)} %pad_maximum_fusion.2), channel_id=1, source_target_pairs={{0,8},{8,0},{16,24},{24,16},{1,9},{9,1},{17,25},{25,17},{2,10},{10... | collective-permute-start | bytes 6291464 | tf_op jit(solution)/shard_map/ppermute | solution.py:32
  37.0 33.7 %copy-start.4 = (bf16[4,512,512]{2,1,0:T(8,128)(2,1)}, bf16[4,512,512]{2,1,0:T(8,128)(2,1)S(1)}, u32[]{:S(2)}) copy-start(bf16[4,512,512]{2,1,0:T(8,128)(2,1)S(1)} %fusion.22) | copy-start | bytes 6291460
  37.4 132.8 %copy-start.30 = (s32[4]{0:T(128)S(1)}, s32[4]{0:T(128)}, u32[]{:S(2)}) copy-start(s32[4]{0:T(128)} %constant.209.clone) | copy-start | bytes 52
  37.4 134.0 %copy-start.29 = (s32[4]{0:T(128)S(1)}, s32[4]{0:T(128)}, u32[]{:S(2)}) copy-start(s32[4]{0:T(128)} %constant.206.clone) | copy-start | bytes 52
  37.4 135.2 %copy-start.28 = (s32[4]{0:T(128)S(1)}, s32[4]{0:T(128)}, u32[]{:S(2)}) copy-start(s32[4]{0:T(128)} %constant.203.clone) | copy-start | bytes 52
  37.4 136.4 %copy-start.24 = (f32[1024]{0:T(1024)S(1)}, f32[1024]{0:T(1024)}, u32[]{:S(2)}) copy-start(f32[1024]{0:T(1024)} %param.17) | copy-start | bytes 12292
  37.4 136.4 %copy-start.21 = (f32[16]{0:T(128)S(1)}, f32[16]{0:T(128)}, u32[]{:S(2)}) copy-start(f32[16]{0:T(128)} %param.16) | copy-start | bytes 196
  37.4 136.6 %copy-start.27 = (s32[2]{0:T(128)S(1)}, s32[2]{0:T(128)}, u32[]{:S(2)}) copy-start(s32[2]{0:T(128)} %constant.204.clone) | copy-start | bytes 28
  37.5 137.2 %copy-start.26 = (s32[3]{0:T(128)S(1)}, s32[3]{0:T(128)}, u32[]{:S(2)}) copy-start(s32[3]{0:T(128)} %constant.202.clone) | copy-start | bytes 40
  37.5 14.3 %collective-permute-start.4 = (bf16[4,512,128]{2,1,0:T(8,128)(2,1)S(1)}, bf16[4,512,128]{2,1,0:T(8,128)(2,1)S(1)}, u32[]{:S(2)}, u32[]{:S(2)}) collective-permute-start(bf16[4,512,128]{2,1,0:T(8,128)(2,1)S(1)} %get-tuple-element.61), channel_id=1, source_target_pairs={{0,17},{1,16},{8,25},{9,24},{16,1},{17,0},{24,9},{25,8},{2,19},{3,... | collective-permute-start | bytes 1572872 | tf_op jit(solution)/shard_map/ppermute | solution.py:28
  40.0 23.6 %collective-permute-start.3 = (bf16[4,512,128]{2,1,0:T(8,128)(2,1)S(1)}, bf16[4,512,128]{2,1,0:T(8,128)(2,1)S(1)}, u32[]{:S(2)}, u32[]{:S(2)}) collective-permute-start(bf16[4,512,128]{2,1,0:T(8,128)(2,1)S(1)} %get-tuple-element.62), channel_id=1, source_target_pairs={{0,1},{1,0},{8,9},{9,8},{16,17},{17,16},{24,25},{25,24},{2,3},{3,2... | collective-permute-start | bytes 1572872 | tf_op jit(solution)/shard_map/ppermute | solution.py:28
  40.2 23.4 %collective-permute-start.2 = (bf16[4,512,128]{2,1,0:T(8,128)(2,1)S(1)}, bf16[4,512,128]{2,1,0:T(8,128)(2,1)S(1)}, u32[]{:S(2)}, u32[]{:S(2)}) collective-permute-start(bf16[4,512,128]{2,1,0:T(8,128)(2,1)S(1)} %get-tuple-element.63), channel_id=1, source_target_pairs={{0,16},{1,17},{8,24},{9,25},{16,0},{17,1},{24,8},{25,9},{2,18},{3,... | collective-permute-start | bytes 1572872 | tf_op jit(solution)/shard_map/ppermute | solution.py:28
  63.7 46.4 %collective-permute-start.8 = (bf16[4,512,512]{2,1,0:T(8,128)(2,1)S(1)}, bf16[4,512,512]{2,1,0:T(8,128)(2,1)S(1)}, u32[]{:S(2)}, u32[]{:S(2)}) collective-permute-start(bf16[4,512,512]{2,1,0:T(8,128)(2,1)S(1)} %fusion.22), channel_id=1, source_target_pairs={{0,1},{1,0},{8,9},{9,8},{16,17},{17,16},{24,25},{25,24},{2,3},{3,2... | collective-permute-start | bytes 6291464 | tf_op jit(solution)/shard_map/ppermute | solution.py:28
  65.2 46.4 %collective-permute-start.7 = (bf16[4,512,512]{2,1,0:T(8,128)(2,1)S(1)}, bf16[4,512,512]{2,1,0:T(8,128)(2,1)S(1)}, u32[]{:S(2)}, u32[]{:S(2)}) collective-permute-start(bf16[4,512,512]{2,1,0:T(8,128)(2,1)S(1)} %fusion.22), channel_id=1, source_target_pairs={{0,16},{1,17},{8,24},{9,25},{16,0},{17,1},{24,8},{25,9},{2,18},{3,... | collective-permute-start | bytes 6291464 | tf_op jit(solution)/shard_map/ppermute | solution.py:28
  65.3 47.6 %collective-permute-start.6 = (bf16[4,2048,128]{2,1,0:T(8,128)(2,1)S(1)}, bf16[4,2048,128]{2,1,0:T(8,128)(2,1)S(1)}, u32[]{:S(2)}, u32[]{:S(2)}) collective-permute-start(bf16[4,2048,128]{2,1,0:T(8,128)(2,1)S(1)} %pad_maximum_fusion.3), channel_id=1, source_target_pairs={{2,0},{4,2},{6,4},{3,1},{5,3},{7,5},{10,8},{12,10},{14,12},{11,9},... | collective-permute-start | bytes 6291464 | tf_op jit(solution)/shard_map/ppermute | solution.py:39
  66.6 47.2 %collective-permute-start.5 = (bf16[4,2048,128]{2,1,0:T(8,128)(2,1)S(1)}, bf16[4,2048,128]{2,1,0:T(8,128)(2,1)S(1)}, u32[]{:S(2)}, u32[]{:S(2)}) collective-permute-start(bf16[4,2048,128]{2,1,0:T(8,128)(2,1)S(1)} %pad_maximum_fusion.3), channel_id=1, source_target_pairs={{0,2},{2,4},{4,6},{1,3},{3,5},{5,7},{8,10},{10,12},{12,14},{9,11},... | collective-permute-start | bytes 6291464 | tf_op jit(solution)/shard_map/ppermute | solution.py:39
  70.7 85.4 %collective-permute-start.11 = (bf16[4,512,512]{2,1,0:T(8,128)(2,1)S(1)}, bf16[4,512,512]{2,1,0:T(8,128)(2,1)S(1)}, u32[]{:S(2)}, u32[]{:S(2)}) collective-permute-start(bf16[4,512,512]{2,1,0:T(8,128)(2,1)S(1)} %fusion.22), channel_id=1, source_target_pairs={{0,17},{1,16},{8,25},{9,24},{16,1},{17,0},{24,9},{25,8},{2,19},{3,... | collective-permute-start | bytes 6291464 | tf_op jit(solution)/shard_map/ppermute | solution.py:28
  110.2 58.2 %copy-start.11 = (bf16[4,512,512]{2,1,0:T(8,128)(2,1)}, bf16[4,512,512]{2,1,0:T(8,128)(2,1)S(1)}, u32[]{:S(2)}) copy-start(bf16[4,512,512]{2,1,0:T(8,128)(2,1)S(1)} %collective-permute-done.8) | copy-start | bytes 6291460
  111.6 56.8 %copy-start.13 = (bf16[4,512,512]{2,1,0:T(8,128)(2,1)}, bf16[4,512,512]{2,1,0:T(8,128)(2,1)S(1)}, u32[]{:S(2)}) copy-start(bf16[4,512,512]{2,1,0:T(8,128)(2,1)S(1)} %collective-permute-done.7) | copy-start | bytes 6291460
  112.9 43.2 %copy-start.7 = (bf16[4,2048,128]{2,1,0:T(8,128)(2,1)}, bf16[4,2048,128]{2,1,0:T(8,128)(2,1)S(1)}, u32[]{:S(2)}) copy-start(bf16[4,2048,128]{2,1,0:T(8,128)(2,1)S(1)} %collective-permute-done.6) | copy-start | bytes 6291460
  113.8 51.7 %copy-start.8 = (bf16[4,2048,128]{2,1,0:T(8,128)(2,1)}, bf16[4,2048,128]{2,1,0:T(8,128)(2,1)S(1)}, u32[]{:S(2)}) copy-start(bf16[4,2048,128]{2,1,0:T(8,128)(2,1)S(1)} %collective-permute-done.5) | copy-start | bytes 6291460
  113.8 46.4 %collective-permute-start.9 = (bf16[4,2048,128]{2,1,0:T(8,128)(2,1)S(1)}, bf16[4,2048,128]{2,1,0:T(8,128)(2,1)}, u32[]{:S(2)}, u32[]{:S(2)}) collective-permute-start(bf16[4,2048,128]{2,1,0:T(8,128)(2,1)S(1)} %collective-permute-done.5), channel_id=1, source_target_pairs={{0,2},{2,4},{4,6},{1,3},{3,5},{5,7},{8,10},{10,12},{12,14},{9,11},... | collective-permute-start | bytes 6291464 | tf_op jit(solution)/shard_map/ppermute | solution.py:39
  119.3 46.2 %collective-permute-start.10 = (bf16[4,2048,128]{2,1,0:T(8,128)(2,1)S(1)}, bf16[4,2048,128]{2,1,0:T(8,128)(2,1)}, u32[]{:S(2)}, u32[]{:S(2)}) collective-permute-start(bf16[4,2048,128]{2,1,0:T(8,128)(2,1)S(1)} %collective-permute-done.6), channel_id=1, source_target_pairs={{2,0},{4,2},{6,4},{3,1},{5,3},{7,5},{10,8},{12,10},{14,12},{11,9},... | collective-permute-start | bytes 6291464 | tf_op jit(solution)/shard_map/ppermute | solution.py:39
  156.1 12.3 %copy-start.15 = (bf16[4,512,512]{2,1,0:T(8,128)(2,1)}, bf16[4,512,512]{2,1,0:T(8,128)(2,1)S(1)}, u32[]{:S(2)}) copy-start(bf16[4,512,512]{2,1,0:T(8,128)(2,1)S(1)} %collective-permute-done.11) | copy-start | bytes 6291460
  165.5 42.9 %collective-permute-start.15 = (bf16[4,2048,128]{2,1,0:T(8,128)(2,1)}, bf16[4,2048,128]{2,1,0:T(8,128)(2,1)}, u32[]{:S(2)}, u32[]{:S(2)}) collective-permute-start(bf16[4,2048,128]{2,1,0:T(8,128)(2,1)} %collective-permute-done.9), channel_id=1, source_target_pairs={{0,2},{2,4},{4,6},{1,3},{3,5},{5,7},{8,10},{10,12},{12,14},{9,11},... | collective-permute-start | bytes 6291464 | tf_op jit(solution)/shard_map/ppermute | solution.py:39
  168.4 45.1 %collective-permute-start.16 = (bf16[4,2048,128]{2,1,0:T(8,128)(2,1)}, bf16[4,2048,128]{2,1,0:T(8,128)(2,1)}, u32[]{:S(2)}, u32[]{:S(2)}) collective-permute-start(bf16[4,2048,128]{2,1,0:T(8,128)(2,1)} %collective-permute-done.10), channel_id=1, source_target_pairs={{2,0},{4,2},{6,4},{3,1},{5,3},{7,5},{10,8},{12,10},{14,12},{11,9},... | collective-permute-start | bytes 6291464 | tf_op jit(solution)/shard_map/ppermute | solution.py:39
  178.5 46.2 %copy-start.5 = (bf16[4,512,512]{2,1,0:T(8,128)(2,1)S(1)}, bf16[4,512,512]{2,1,0:T(8,128)(2,1)}, u32[]{:S(2)}) copy-start(bf16[4,512,512]{2,1,0:T(8,128)(2,1)} %copy-done.4) | copy-start | bytes 6291460
  178.5 56.1 %collective-permute-start.12 = (bf16[4,2048,128]{2,1,0:T(8,128)(2,1)S(1)}, bf16[4,2048,128]{2,1,0:T(8,128)(2,1)S(1)}, u32[]{:S(2)}, u32[]{:S(2)}) collective-permute-start(bf16[4,2048,128]{2,1,0:T(8,128)(2,1)S(1)} %pad_maximum_fusion.3), channel_id=1, source_target_pairs={{0,8},{8,0},{16,24},{24,16},{1,9},{9,1},{17,25},{25,17},{2,10},{10... | collective-permute-start | bytes 6291464 | tf_op jit(solution)/shard_map/ppermute | solution.py:32
  218.5 15.0 %copy-start.9 = (bf16[4,2048,128]{2,1,0:T(8,128)(2,1)}, bf16[4,2048,128]{2,1,0:T(8,128)(2,1)S(1)}, u32[]{:S(2)}) copy-start(bf16[4,2048,128]{2,1,0:T(8,128)(2,1)S(1)} %get-tuple-element.51) | copy-start | bytes 6291460
  218.5 6.3 %copy-start.14 = (bf16[4,512,512]{2,1,0:T(8,128)(2,1)S(1)}, bf16[4,512,512]{2,1,0:T(8,128)(2,1)}, u32[]{:S(2)}) copy-start(bf16[4,512,512]{2,1,0:T(8,128)(2,1)} %copy-done.13) | copy-start | bytes 6291460
  218.5 16.1 %collective-permute-start.14 = (bf16[4,2048,128]{2,1,0:T(8,128)(2,1)S(1)}, bf16[4,2048,128]{2,1,0:T(8,128)(2,1)S(1)}, u32[]{:S(2)}, u32[]{:S(2)}) collective-permute-start(bf16[4,2048,128]{2,1,0:T(8,128)(2,1)S(1)} %get-tuple-element.52), channel_id=1, source_target_pairs={{0,8},{8,0},{16,24},{24,16},{1,9},{9,1},{17,25},{25,17},{2,10},{10... | collective-permute-start | bytes 6291464 | tf_op jit(solution)/shard_map/ppermute | solution.py:32
  223.7 10.9 %collective-permute-start.13 = (bf16[4,2048,128]{2,1,0:T(8,128)(2,1)S(1)}, bf16[4,2048,128]{2,1,0:T(8,128)(2,1)}, u32[]{:S(2)}, u32[]{:S(2)}) collective-permute-start(bf16[4,2048,128]{2,1,0:T(8,128)(2,1)S(1)} %get-tuple-element.53), channel_id=1, source_target_pairs={{0,8},{8,0},{16,24},{24,16},{1,9},{9,1},{17,25},{25,17},{2,10},{10... | collective-permute-start | bytes 6291464 | tf_op jit(solution)/shard_map/ppermute | solution.py:32
  228.2 5.3 %copy-start.3 = (bf16[4,2048,512]{2,1,0:T(8,128)(2,1)}, bf16[4,2048,512]{2,1,0:T(8,128)(2,1)S(1)}, u32[]{:S(2)}) copy-start(bf16[4,2048,512]{2,1,0:T(8,128)(2,1)S(1)} %constant_dynamic-update-slice_fusion) | copy-start | bytes 25165828
  233.4 46.7 %collective-permute-start.17 = (bf16[4,2048,128]{2,1,0:T(8,128)(2,1)S(1)}, bf16[4,2048,128]{2,1,0:T(8,128)(2,1)S(1)}, u32[]{:S(2)}, u32[]{:S(2)}) collective-permute-start(bf16[4,2048,128]{2,1,0:T(8,128)(2,1)S(1)} %get-tuple-element.51), channel_id=1, source_target_pairs={{0,8},{8,0},{16,24},{24,16},{1,9},{9,1},{17,25},{25,17},{2,10},{10... | collective-permute-start | bytes 6291464 | tf_op jit(solution)/shard_map/ppermute | solution.py:32
  239.8 34.3 %copy-start.2 = (bf16[12,2048,256]{2,1,0:T(8,128)(2,1)}, bf16[12,2048,256]{2,1,0:T(8,128)(2,1)S(1)}, u32[]{:S(2)}) copy-start(bf16[12,2048,256]{2,1,0:T(8,128)(2,1)S(1)} %maximum_maximum_fusion) | copy-start | bytes 37748740
  329.8 51.2 %collective-permute-start.18 = (bf16[2,512,512]{2,1,0:T(8,128)(2,1)}, bf16[2,512,512]{2,1,0:T(8,128)(2,1)}, u32[]{:S(2)}, u32[]{:S(2)}) collective-permute-start(bf16[2,512,512]{2,1,0:T(8,128)(2,1)} %bitcast.15), channel_id=1, source_target_pairs={{0,1},{1,0},{8,9},{9,8},{16,17},{17,16},{24,25},{25,24},{2,3},{3,2... | collective-permute-start | bytes 3145736 | tf_op jit(solution)/shard_map/ppermute | solution.py:28
  332.0 52.4 %collective-permute-start.21 = (bf16[2,512,512]{2,1,0:T(8,128)(2,1)}, bf16[2,512,512]{2,1,0:T(8,128)(2,1)S(1)}, u32[]{:S(2)}, u32[]{:S(2)}) collective-permute-start(bf16[2,512,512]{2,1,0:T(8,128)(2,1)} %bitcast.24), channel_id=1, source_target_pairs={{0,1},{1,0},{8,9},{9,8},{16,17},{17,16},{24,25},{25,24},{2,3},{3,2... | collective-permute-start | bytes 3145736 | tf_op jit(solution)/shard_map/ppermute | solution.py:28
  377.6 24.5 %collective-permute-start.27 = (bf16[2,512,512]{2,1,0:T(8,128)(2,1)S(1)}, bf16[2,512,512]{2,1,0:T(8,128)(2,1)S(1)}, u32[]{:S(2)}, u32[]{:S(2)}) collective-permute-start(bf16[2,512,512]{2,1,0:T(8,128)(2,1)S(1)} %bitcast.116), channel_id=1, source_target_pairs={{0,1},{1,0},{8,9},{9,8},{16,17},{17,16},{24,25},{25,24},{2,3},{3,2... | collective-permute-start | bytes 3145736 | tf_op jit(solution)/shard_map/ppermute | solution.py:28
  380.8 43.8 %collective-permute-start.24 = (bf16[2,512,512]{2,1,0:T(8,128)(2,1)S(1)}, bf16[2,512,512]{2,1,0:T(8,128)(2,1)S(1)}, u32[]{:S(2)}, u32[]{:S(2)}) collective-permute-start(bf16[2,512,512]{2,1,0:T(8,128)(2,1)S(1)} %bitcast.115), channel_id=1, source_target_pairs={{0,1},{1,0},{8,9},{9,8},{16,17},{17,16},{24,25},{25,24},{2,3},{3,2... | collective-permute-start | bytes 3145736 | tf_op jit(solution)/shard_map/ppermute | solution.py:28
  382.6 43.7 %collective-permute-start.19 = (bf16[2,512,512]{2,1,0:T(8,128)(2,1)S(1)}, bf16[2,512,512]{2,1,0:T(8,128)(2,1)S(1)}, u32[]{:S(2)}, u32[]{:S(2)}) collective-permute-start(bf16[2,512,512]{2,1,0:T(8,128)(2,1)S(1)} %fusion.31), channel_id=1, source_target_pairs={{0,16},{1,17},{8,24},{9,25},{16,0},{17,1},{24,8},{25,9},{2,18},{3,... | collective-permute-start | bytes 3145736 | tf_op jit(solution)/shard_map/ppermute | solution.py:28
  384.8 46.0 %collective-permute-start.22 = (bf16[2,512,512]{2,1,0:T(8,128)(2,1)S(1)}, bf16[2,512,512]{2,1,0:T(8,128)(2,1)S(1)}, u32[]{:S(2)}, u32[]{:S(2)}) collective-permute-start(bf16[2,512,512]{2,1,0:T(8,128)(2,1)S(1)} %fusion.32), channel_id=1, source_target_pairs={{0,16},{1,17},{8,24},{9,25},{16,0},{17,1},{24,8},{25,9},{2,18},{3,... | collective-permute-start | bytes 3145736 | tf_op jit(solution)/shard_map/ppermute | solution.py:28
  402.4 49.1 %collective-permute-start.28 = (bf16[2,512,512]{2,1,0:T(8,128)(2,1)S(1)}, bf16[2,512,512]{2,1,0:T(8,128)(2,1)S(1)}, u32[]{:S(2)}, u32[]{:S(2)}) collective-permute-start(bf16[2,512,512]{2,1,0:T(8,128)(2,1)S(1)} %fusion.34), channel_id=1, source_target_pairs={{0,16},{1,17},{8,24},{9,25},{16,0},{17,1},{24,8},{25,9},{2,18},{3,... | collective-permute-start | bytes 3145736 | tf_op jit(solution)/shard_map/ppermute | solution.py:28
  424.9 49.1 %collective-permute-start.25 = (bf16[2,512,512]{2,1,0:T(8,128)(2,1)S(1)}, bf16[2,512,512]{2,1,0:T(8,128)(2,1)S(1)}, u32[]{:S(2)}, u32[]{:S(2)}) collective-permute-start(bf16[2,512,512]{2,1,0:T(8,128)(2,1)S(1)} %fusion.33), channel_id=1, source_target_pairs={{0,16},{1,17},{8,24},{9,25},{16,0},{17,1},{24,8},{25,9},{2,18},{3,... | collective-permute-start | bytes 3145736 | tf_op jit(solution)/shard_map/ppermute | solution.py:28
  429.1 48.1 %collective-permute-start.20 = (bf16[2,512,512]{2,1,0:T(8,128)(2,1)}, bf16[2,512,512]{2,1,0:T(8,128)(2,1)}, u32[]{:S(2)}, u32[]{:S(2)}) collective-permute-start(bf16[2,512,512]{2,1,0:T(8,128)(2,1)} %add_convert_fusion.3), channel_id=1, source_target_pairs={{0,8},{8,0},{16,24},{24,16},{1,9},{9,1},{17,25},{25,17},{2,10},{10... | collective-permute-start | bytes 3145736 | tf_op jit(solution)/shard_map/ppermute | solution.py:32
  432.3 46.7 %collective-permute-start.23 = (bf16[2,512,512]{2,1,0:T(8,128)(2,1)}, bf16[2,512,512]{2,1,0:T(8,128)(2,1)}, u32[]{:S(2)}, u32[]{:S(2)}) collective-permute-start(bf16[2,512,512]{2,1,0:T(8,128)(2,1)} %add_convert_fusion.2), channel_id=1, source_target_pairs={{0,8},{8,0},{16,24},{24,16},{1,9},{9,1},{17,25},{25,17},{2,10},{10... | collective-permute-start | bytes 3145736 | tf_op jit(solution)/shard_map/ppermute | solution.py:32
  452.0 28.8 %collective-permute-start.29 = (bf16[2,512,512]{2,1,0:T(8,128)(2,1)S(1)}, bf16[2,512,512]{2,1,0:T(8,128)(2,1)}, u32[]{:S(2)}, u32[]{:S(2)}) collective-permute-start(bf16[2,512,512]{2,1,0:T(8,128)(2,1)S(1)} %add_convert_fusion), channel_id=1, source_target_pairs={{0,8},{8,0},{16,24},{24,16},{1,9},{9,1},{17,25},{25,17},{2,10},{10... | collective-permute-start | bytes 3145736 | tf_op jit(solution)/shard_map/ppermute | solution.py:32
  475.5 6.8 %collective-permute-start.26 = (bf16[2,512,512]{2,1,0:T(8,128)(2,1)}, bf16[2,512,512]{2,1,0:T(8,128)(2,1)S(1)}, u32[]{:S(2)}, u32[]{:S(2)}) collective-permute-start(bf16[2,512,512]{2,1,0:T(8,128)(2,1)} %add_convert_fusion.1), channel_id=1, source_target_pairs={{0,8},{8,0},{16,24},{24,16},{1,9},{9,1},{17,25},{25,17},{2,10},{10... | collective-permute-start | bytes 3145736 | tf_op jit(solution)/shard_map/ppermute | solution.py:32
  (13 other events, 33.9 us)

commit v3 on v2

--- a/solution.py
+++ b/solution.py
@@ -132,12 +132,15 @@
         early_keys = jnp.concatenate([k for k, _ in early], 0)
         early_energy = jnp.concatenate([e for _, e in early], 0)
         early_amplitude = amplitudes(queries, own_energy, early_keys, early_energy)
+        up[-1], down[-1], early_amplitude = lax.optimization_barrier((up[-1], down[-1], early_amplitude))
     visiting, visit_energy = stage_keys(blk_size - 1)
     parts, wide = [], []
     for i in range(occ_block):
         rows, before = queries[i : i + 1], None if early_amplitude is None else early_amplitude[i]
         if parts:
             rows, before, parts[-1] = lax.optimization_barrier((rows, before, parts[-1]))
+        if i > 1:
+            rows, before, wide[i - 2] = lax.optimization_barrier((rows, before, wide[i - 2]))
         part = contracted(amplitudes(rows, own_energy[i : i + 1], visiting, visit_energy)[0], visiting)
         if before is not None:
             part = part + contracted(before, early_keys)

time: 503 us -> 474 us (0.942)
  waiting for transfers between devices: 237 us -> 193 us
  starting transfers between devices: 54.3 us -> 64.7 us
    ppermute x15, waiting for transfers between devices: 194 us -> 147 us  [plane_shift(): return lax.ppermute(v, ('sec', 'aux'), perm)]
    ppermute x9, starting transfers between devices: 20 us -> 30.1 us  [core_shift(): return lax.ppermute(v, 'sec', perm)]
    unnamed x65 -> x61, local copies, waits for them, and re-layouts: 10.6 us -> 9.78 us
  transfers between devices with their start and end apart: 30 -> 30, of which waited for: 17 -> 17; matrix products, arithmetic and copies ran while one was open for 25% -> 27% of each run, Pallas kernels for 0% -> 0%
where the time goes in v3:
time: 474 us; the launch traced here: 467 us
  waiting for transfers between devices  193 us (41%)
  matrix products  127 us (27%)
  starting transfers between devices  64.7 us (14%)
  local copies, waits for them, and re-layouts  43.9 us (9%)
  other arithmetic  35.8 us (8%)
    ppermute x15, waiting for transfers between devices, plane_shift(): return lax.ppermute(v, ('sec', 'aux'), perm)  147 us
    dot_general x8, matrix products, contracted(): jnp.einsum('ajb,jpb->pa', amplitude, visiting, preferred_element_type=jnp...  86.1 us
    ppermute x6, waiting for transfers between devices, line(): return lax.ppermute(v, 'blk', perm)  45.4 us
    dot_general x1, matrix products, amplitudes(): jnp.einsum('ipa,jpb->iajb', rows, visiting, preferred_element_type=jnp.fl...  31.3 us
    ppermute x9, starting transfers between devices, core_shift(): return lax.ppermute(v, 'sec', perm)  30.1 us
    ppermute x6, starting transfers between devices, line(): return lax.ppermute(v, 'blk', perm)  17.6 us
    ppermute x15, starting transfers between devices, plane_shift(): return lax.ppermute(v, ('sec', 'aux'), perm)  17 us
    unnamed x61, local copies, waits for them, and re-layouts  9.78 us
  transfers between devices with their start and end apart: 30, of which 17 were waited for; matrix products, arithmetic and copies ran while one was open for 27% of the time, Pallas kernels for 0%

profile of v3, /device:TPU:1, one launch (start us, length us, event | category | flops | bytes accessed | tf_op | source)
XLA Modules:
  0.0 467.4 jit_solution(10864371611484262022)
XLA Ops:
  1.7 2.1 collective-permute-start
  3.8 22.9 %collective-permute-done = bf16[4,512,256]{2,1,0:T(8,128)(2,1)S(1)} collective-permute-done((bf16[4,512,256]{2,1,0:T(8,128)(2,1)S(1)}, bf16[4,512,256]{2,1,0:T(8,128)(2,1)S(1)}, u32[]{:S(2)}, u32[]{:S(2)}) %collective-permute-start) | collective-permute-done | bytes 1048608 | tf_op jit(solution)/shard_map/ppermute | solution.py:28
  29.1 3.4 fusion.62
  33.0 5.3 %fusion.24 = bf16[4,512,512]{2,1,0:T(8,128)(2,1)} fusion(bf16[4,512,512]{2,1,0:T(8,128)(2,1)} %collective-permute-done.1, bf16[4,512,256]{2,1,0:T(8,128)(2,1)S(1)} %copy-done.15, bf16[4,512,256]{2,1,0:T(8,128)(2,1)S(1)} %get-tuple-element.81, bf16[256,512]{1,0:T(8,128)(2,1)S(1)} %get-tuple-element.73, bf16[256,512]{1,0:T(8,128)(2,1)S(1)} %get-tuple-element.74, ...), kind=kOutput, calls=%fused_computation.61 | convolution fusion | flops 2165309440 | bytes 7340032 | tf_op jit(solution)/shard_map/ipm,ma->ipa/dot_general | solution.py:53
  40.0 2.5 collective-permute-start.4
  42.9 11.4 %collective-permute-done.4 = bf16[4,512,128]{2,1,0:T(8,128)(2,1)S(1)} collective-permute-done((bf16[4,512,128]{2,1,0:T(8,128)(2,1)S(1)}, bf16[4,512,128]{2,1,0:T(8,128)(2,1)S(1)}, u32[]{:S(2)}, u32[]{:S(2)}) %collective-permute-start.4) | collective-permute-done | bytes 524320 | tf_op jit(solution)/shard_map/ppermute | solution.py:28
  54.3 11.8 %collective-permute-done.3 = bf16[4,512,128]{2,1,0:T(8,128)(2,1)S(1)} collective-permute-done((bf16[4,512,128]{2,1,0:T(8,128)(2,1)S(1)}, bf16[4,512,128]{2,1,0:T(8,128)(2,1)S(1)}, u32[]{:S(2)}, u32[]{:S(2)}) %collective-permute-start.3) | collective-permute-done | bytes 524320 | tf_op jit(solution)/shard_map/ppermute | solution.py:28
  70.3 5.3 %collective-permute-start.5 = (bf16[4,2048,128]{2,1,0:T(8,128)(2,1)}, bf16[4,2048,128]{2,1,0:T(8,128)(2,1)}, u32[]{:S(2)}, u32[]{:S(2)}) collective-permute-start(bf16[4,2048,128]{2,1,0:T(8,128)(2,1)} %pad_maximum_fusion.3), channel_id=1, source_target_pairs={{0,2},{2,4},{4,6},{1,3},{3,5},{5,7},{8,10},{10,12},{12,14},{9,11},... | collective-permute-start | bytes 6291464 | tf_op jit(solution)/shard_map/ppermute | solution.py:39
  75.6 38.7 %collective-permute-done.8 = bf16[4,512,512]{2,1,0:T(8,128)(2,1)S(1)} collective-permute-done((bf16[4,512,512]{2,1,0:T(8,128)(2,1)}, bf16[4,512,512]{2,1,0:T(8,128)(2,1)S(1)}, u32[]{:S(2)}, u32[]{:S(2)}) %collective-permute-start.8) | collective-permute-done | bytes 2097184 | tf_op jit(solution)/shard_map/ppermute | solution.py:28
  117.8 4.2 collective-permute-start.9
  126.1 3.1 collective-permute-start.14
  129.2 35.3 %collective-permute-done.9 = bf16[4,2048,128]{2,1,0:T(8,128)(2,1)S(1)} collective-permute-done((bf16[4,2048,128]{2,1,0:T(8,128)(2,1)}, bf16[4,2048,128]{2,1,0:T(8,128)(2,1)S(1)}, u32[]{:S(2)}, u32[]{:S(2)}) %collective-permute-start.9) | collective-permute-done | bytes 2097184 | tf_op jit(solution)/shard_map/ppermute | solution.py:39
  165.8 2.6 collective-permute-done.10
  168.5 5.2 %broadcast_select_fusion = (bf16[4,2048,128]{2,1,0:T(8,128)(2,1)S(1)}, bf16[4,2048,128]{2,1,0:T(8,128)(2,1)}) fusion(bf16[4,2048,128]{2,1,0:T(8,128)(2,1)} %collective-permute-done.5, bf16[4,2048,128]{2,1,0:T(8,128)(2,1)} %collective-permute-done.6, pred[]{:T(512)} %compare_reduce_fusion.1, bf16[4,2048,128]{2,1,0:T(8,128)(2,1)} %copy-done.4, ...), kind=kLoop, calls=%fused_computation.60 | loop fusion | flops 3145728 | bytes 12582915 | tf_op jit(solution)/shard_map/jit(_where)/select_n | solution.py:111
  173.6 3.8 collective-permute-start.15
  182.9 1.9 constant_dynamic-update-slice_fusion.3
  186.7 4.2 collective-permute-start.12
  192.2 1.7 constant_dynamic-update-slice_fusion
  194.0 8.8 %maximum_maximum_fusion = bf16[12,2048,256]{2,1,0:T(8,128)(2,1)S(1)} fusion(bf16[4,2048,128]{2,1,0:T(8,128)(2,1)} %collective-permute-done.16, bf16[4,2048,128]{2,1,0:T(8,128)(2,1)} %get-tuple-element.76, bf16[4,2048,128]{2,1,0:T(8,128)(2,1)} %collective-permute-done.15, bf16[4,2048,128]{2,1,0:T(8,128)(2,1)S(1)} %get-tuple-element.75, ...), kind=kLoop, calls=%fused_computation.1 | loop fusion | flops 75497472 | bytes 25165824 | tf_op jit(solution)/shard_map/concatenate | solution.py:132
  202.8 31.3 %divide_convert_fusion = bf16[4,512,12,256]{3,1,2,0:T(8,128)(2,1)} fusion(bf16[12,2048,256]{2,1,0:T(8,128)(2,1)S(1)} %maximum_maximum_fusion, f32[256]{0:T(256)S(1)} %pad_maximum_fusion.4, f32[4,512,12]{1,2,0:T(8,128)S(1)} %broadcast_subtract_fusion, bf16[4,2048,512]{2,1,0:T(8,128)(2,1)S(1)} %constant_dynamic-update-slice_fusion), kind=kOutput, calls=%fused_computation | convolution fusion | flops 25794969600 | bytes 33653760 | tf_op jit(solution)/shard_map/ipa,jpb->iajb/dot_general | solution.py:117
  235.3 4.2 collective-permute-done.13
  239.5 2.4 select_select_fusion
  241.9 1.7 collective-permute-start.17
  243.6 1.9 broadcast_add_fusion.2
  245.6 3.3 fusion.61
  250.0 3.8 slice_bitcast_fusion.2
  255.1 9.4 %fusion.43 = f32[2048,512,1]{1,0,2:T(8,128)} fusion(bf16[4,2048,512]{2,1,0:T(8,128)(2,1)} %copy-done.3, f32[256]{0:T(256)S(1)} %pad_maximum_fusion.4, f32[512,4]{0,1:T(4,128)S(1)} %get-tuple-element.96, bf16[4,2048,128]{2,1,0:T(8,128)(2,1)} %copy-done.20, bf16[4,2048,128]{2,1,0:T(8,128)(2,1)S(1)} %select_select_fusion), kind=kOutput, calls=%fused_computation.73 | convolution fusion | flops 4313841664 | bytes 14689280 | tf_op jit(solution)/shard_map/ajb,jpb->pa/dot_general | solution.py:127
  264.5 11.4 %bitcast_add_fusion.3 = f32[2048,512]{1,0:T(8,128)S(1)} fusion(f32[2048,512,1]{1,0,2:T(8,128)} %fusion.43, bf16[12,2048,256]{2,1,0:T(8,128)(2,1)} %copy-done.2, bf16[4,512,12,256]{3,1,2,0:T(8,128)(2,1)} %divide_convert_fusion), kind=kOutput, calls=%fused_computation.20 | convolution fusion | flops 6443499520 | bytes 24117248 | tf_op jit(solution)/shard_map/ajb,jpb->pa/dot_general | solution.py:127
  278.5 1.8 collective-permute-start.18
  280.4 9.4 %fusion.45 = f32[2048,512,1]{1,0,2:T(8,128)} fusion(bf16[1,2048,512]{2,1,0:T(8,128)(2,1)} %get-tuple-element.45, f32[512,4]{0,1:T(4,128)S(1)} %get-tuple-element.94, f32[256]{0:T(256)S(1)} %pad_maximum_fusion.4, bf16[4,2048,128]{2,1,0:T(8,128)(2,1)} %copy-done.20, bf16[4,2048,128]{2,1,0:T(8,128)(2,1)S(1)} %select_select_fusion), kind=kOutput, calls=%fused_computation.74 | convolution fusion | flops 4313841664 | bytes 10494976 | tf_op jit(solution)/shard_map/ajb,jpb->pa/dot_general | solution.py:127
  289.8 11.2 %bitcast_add_fusion.2 = f32[2048,512]{1,0:T(8,128)S(1)} fusion(f32[2048,512,1]{1,0,2:T(8,128)} %fusion.45, bf16[12,2048,256]{2,1,0:T(8,128)(2,1)} %copy-done.2, bf16[512,12,256]{2,0,1:T(8,128)(2,1)} %get-tuple-element.46), kind=kOutput, calls=%fused_computation.19 | convolution fusion | flops 6443499520 | bytes 24117248 | tf_op jit(solution)/shard_map/ajb,jpb->pa/dot_general | solution.py:127
  303.7 11.0 %fusion.48 = f32[2048,512,1]{1,0,2:T(8,128)} fusion(bf16[1,2048,512]{2,1,0:T(8,128)(2,1)} %get-tuple-element.51, f32[512,4]{0,1:T(4,128)S(1)} %get-tuple-element.95, f32[256]{0:T(256)S(1)} %pad_maximum_fusion.4, bf16[4,2048,128]{2,1,0:T(8,128)(2,1)} %copy-done.20, bf16[4,2048,128]{2,1,0:T(8,128)(2,1)} %copy-done.13), kind=kOutput, calls=%fused_computation.75 | convolution fusion | flops 4313841664 | bytes 10494976 | tf_op jit(solution)/shard_map/ajb,jpb->pa/dot_general | solution.py:127
  314.7 11.4 %bitcast_add_fusion.1 = f32[2048,512]{1,0:T(8,128)S(1)} fusion(f32[2048,512,1]{1,0,2:T(8,128)} %fusion.48, bf16[12,2048,256]{2,1,0:T(8,128)(2,1)} %copy-done.2, bf16[512,12,256]{2,0,1:T(8,128)(2,1)} %get-tuple-element.52), kind=kOutput, calls=%fused_computation.18 | convolution fusion | flops 6443499520 | bytes 24117248 | tf_op jit(solution)/shard_map/ajb,jpb->pa/dot_general | solution.py:127
  328.1 10.6 %fusion.51 = f32[2048,512,1]{1,0,2:T(8,128)} fusion(bf16[1,2048,512]{2,1,0:T(8,128)(2,1)} %get-tuple-element.57, f32[512,4]{0,1:T(4,128)S(1)} %get-tuple-element.93, f32[256]{0:T(256)S(1)} %pad_maximum_fusion.4, bf16[4,2048,128]{2,1,0:T(8,128)(2,1)} %copy-done.20, bf16[4,2048,128]{2,1,0:T(8,128)(2,1)} %copy-done.13), kind=kOutput, calls=%fused_computation.76 | convolution fusion | flops 4313841664 | bytes 10494976 | tf_op jit(solution)/shard_map/ajb,jpb->pa/dot_general | solution.py:127
  338.7 11.6 %bitcast_add_fusion = f32[2048,512]{1,0:T(8,128)S(1)} fusion(f32[2048,512,1]{1,0,2:T(8,128)} %fusion.51, bf16[12,2048,256]{2,1,0:T(8,128)(2,1)} %copy-done.2, bf16[512,12,256]{2,0,1:T(8,128)(2,1)} %get-tuple-element.58), kind=kOutput, calls=%fused_computation.17 | convolution fusion | flops 6443499520 | bytes 24117248 | tf_op jit(solution)/shard_map/ajb,jpb->pa/dot_general | solution.py:127
  357.6 15.8 %collective-permute-done.27 = bf16[2,512,512]{2,1,0:T(8,128)(2,1)S(1)} collective-permute-done((bf16[2,512,512]{2,1,0:T(8,128)(2,1)S(1)}, bf16[2,512,512]{2,1,0:T(8,128)(2,1)S(1)}, u32[]{:S(2)}, u32[]{:S(2)}) %collective-permute-start.27) | collective-permute-done | bytes 1048608 | tf_op jit(solution)/shard_map/ppermute | solution.py:28
  376.7 5.6 %collective-permute-start.20 = (bf16[2,512,512]{2,1,0:T(8,128)(2,1)}, bf16[2,512,512]{2,1,0:T(8,128)(2,1)}, u32[]{:S(2)}, u32[]{:S(2)}) collective-permute-start(bf16[2,512,512]{2,1,0:T(8,128)(2,1)} %add_convert_fusion.3), channel_id=1, source_target_pairs={{0,8},{8,0},{16,24},{24,16},{1,9},{9,1},{17,25},{25,17},{2,10},{10... | collective-permute-start | bytes 3145736 | tf_op jit(solution)/shard_map/ppermute | solution.py:32
  382.3 13.6 %collective-permute-done.24 = bf16[2,512,512]{2,1,0:T(8,128)(2,1)S(1)} collective-permute-done((bf16[2,512,512]{2,1,0:T(8,128)(2,1)S(1)}, bf16[2,512,512]{2,1,0:T(8,128)(2,1)S(1)}, u32[]{:S(2)}, u32[]{:S(2)}) %collective-permute-start.24) | collective-permute-done | bytes 1048608 | tf_op jit(solution)/shard_map/ppermute | solution.py:28
  399.2 5.5 %collective-permute-start.23 = (bf16[2,512,512]{2,1,0:T(8,128)(2,1)}, bf16[2,512,512]{2,1,0:T(8,128)(2,1)}, u32[]{:S(2)}, u32[]{:S(2)}) collective-permute-start(bf16[2,512,512]{2,1,0:T(8,128)(2,1)} %add_convert_fusion.2), channel_id=1, source_target_pairs={{0,8},{8,0},{16,24},{24,16},{1,9},{9,1},{17,25},{25,17},{2,10},{10... | collective-permute-start | bytes 3145736 | tf_op jit(solution)/shard_map/ppermute | solution.py:32
  404.7 15.1 %collective-permute-done.28 = bf16[2,512,512]{2,1,0:T(8,128)(2,1)S(1)} collective-permute-done((bf16[2,512,512]{2,1,0:T(8,128)(2,1)S(1)}, bf16[2,512,512]{2,1,0:T(8,128)(2,1)S(1)}, u32[]{:S(2)}, u32[]{:S(2)}) %collective-permute-start.28) | collective-permute-done | bytes 1048608 | tf_op jit(solution)/shard_map/ppermute | solution.py:28
  420.3 5.9 %collective-permute-start.29 = (bf16[2,512,512]{2,1,0:T(8,128)(2,1)S(1)}, bf16[2,512,512]{2,1,0:T(8,128)(2,1)}, u32[]{:S(2)}, u32[]{:S(2)}) collective-permute-start(bf16[2,512,512]{2,1,0:T(8,128)(2,1)S(1)} %add_convert_fusion), channel_id=1, source_target_pairs={{0,8},{8,0},{16,24},{24,16},{1,9},{9,1},{17,25},{25,17},{2,10},{10... | collective-permute-start | bytes 3145736 | tf_op jit(solution)/shard_map/ppermute | solution.py:32
  426.2 16.0 %collective-permute-done.25 = bf16[2,512,512]{2,1,0:T(8,128)(2,1)S(1)} collective-permute-done((bf16[2,512,512]{2,1,0:T(8,128)(2,1)S(1)}, bf16[2,512,512]{2,1,0:T(8,128)(2,1)S(1)}, u32[]{:S(2)}, u32[]{:S(2)}) %collective-permute-start.25) | collective-permute-done | bytes 1048608 | tf_op jit(solution)/shard_map/ppermute | solution.py:28
  443.8 3.1 collective-permute-start.26
  446.9 1.8 maximum_bitcast_fusion
  448.7 1.8 maximum_bitcast_fusion.1
  454.6 3.4 dynamic-slice_bitcast_fusion.1
  458.0 4.2 fusion.4
  462.2 4.7 %copy.16 = f32[256,4,1024]{2,1,0:T(4,128)} copy(f32[256,4,1024]{2,0,1:T(8,128)S(1)} %fusion.4) | data formatting | bytes 8388608 | tf_op jit(solution)/shard_map/ma,ipa->mip/dot_general | solution.py:169
  (139 shorter events, 57.2 us)
Async XLA Ops:
  1.7 25.0 %collective-permute-start = (bf16[4,512,256]{2,1,0:T(8,128)(2,1)S(1)}, bf16[4,512,256]{2,1,0:T(8,128)(2,1)S(1)}, u32[]{:S(2)}, u32[]{:S(2)}) collective-permute-start(bf16[4,512,256]{2,1,0:T(8,128)(2,1)S(1)} %get-tuple-element.82), channel_id=1, source_target_pairs={{0,16},{1,17},{8,24},{9,25},{16,0},{17,1},{24,8},{25,9},{2,18},{3,... | collective-permute-start | bytes 3145736 | tf_op jit(solution)/shard_map/ppermute | solution.py:28
  27.8 5.2 %collective-permute-start.1 = (bf16[4,512,512]{2,1,0:T(8,128)(2,1)S(1)}, bf16[4,512,512]{2,1,0:T(8,128)(2,1)}, u32[]{:S(2)}, u32[]{:S(2)}) collective-permute-start(bf16[4,512,512]{2,1,0:T(8,128)(2,1)S(1)} %pad_maximum_fusion.2), channel_id=1, source_target_pairs={{0,8},{8,0},{16,24},{24,16},{1,9},{9,1},{17,25},{25,17},{2,10},{10... | collective-permute-start | bytes 6291464 | tf_op jit(solution)/shard_map/ppermute | solution.py:32
  29.1 3.9 copy-start.15
  40.0 83.4 %copy-start.25 = (s32[2]{0:T(128)S(1)}, s32[2]{0:T(128)}, u32[]{:S(2)}) copy-start(s32[2]{0:T(128)} %constant.204.clone) | copy-start | bytes 28
  40.0 84.0 %copy-start.24 = (s32[3]{0:T(128)S(1)}, s32[3]{0:T(128)}, u32[]{:S(2)}) copy-start(s32[3]{0:T(128)} %constant.202.clone) | copy-start | bytes 40
  40.0 14.3 %collective-permute-start.4 = (bf16[4,512,128]{2,1,0:T(8,128)(2,1)S(1)}, bf16[4,512,128]{2,1,0:T(8,128)(2,1)S(1)}, u32[]{:S(2)}, u32[]{:S(2)}) collective-permute-start(bf16[4,512,128]{2,1,0:T(8,128)(2,1)S(1)} %get-tuple-element.78), channel_id=1, source_target_pairs={{0,17},{1,16},{8,25},{9,24},{16,1},{17,0},{24,9},{25,8},{2,19},{3,... | collective-permute-start | bytes 1572872 | tf_op jit(solution)/shard_map/ppermute | solution.py:28
  42.5 23.6 %collective-permute-start.3 = (bf16[4,512,128]{2,1,0:T(8,128)(2,1)S(1)}, bf16[4,512,128]{2,1,0:T(8,128)(2,1)S(1)}, u32[]{:S(2)}, u32[]{:S(2)}) collective-permute-start(bf16[4,512,128]{2,1,0:T(8,128)(2,1)S(1)} %get-tuple-element.79), channel_id=1, source_target_pairs={{0,1},{1,0},{8,9},{9,8},{16,17},{17,16},{24,25},{25,24},{2,3},{3,2... | collective-permute-start | bytes 1572872 | tf_op jit(solution)/shard_map/ppermute | solution.py:28
  42.8 23.4 %collective-permute-start.2 = (bf16[4,512,128]{2,1,0:T(8,128)(2,1)S(1)}, bf16[4,512,128]{2,1,0:T(8,128)(2,1)S(1)}, u32[]{:S(2)}, u32[]{:S(2)}) collective-permute-start(bf16[4,512,128]{2,1,0:T(8,128)(2,1)S(1)} %get-tuple-element.80), channel_id=1, source_target_pairs={{0,16},{1,17},{8,24},{9,25},{16,0},{17,1},{24,8},{25,9},{2,18},{3,... | collective-permute-start | bytes 1572872 | tf_op jit(solution)/shard_map/ppermute | solution.py:28
  67.6 46.7 %collective-permute-start.8 = (bf16[4,512,512]{2,1,0:T(8,128)(2,1)}, bf16[4,512,512]{2,1,0:T(8,128)(2,1)S(1)}, u32[]{:S(2)}, u32[]{:S(2)}) collective-permute-start(bf16[4,512,512]{2,1,0:T(8,128)(2,1)} %fusion.24), channel_id=1, source_target_pairs={{0,1},{1,0},{8,9},{9,8},{16,17},{17,16},{24,25},{25,24},{2,3},{3,2... | collective-permute-start | bytes 6291464 | tf_op jit(solution)/shard_map/ppermute | solution.py:28
  69.1 46.7 %collective-permute-start.7 = (bf16[4,512,512]{2,1,0:T(8,128)(2,1)}, bf16[4,512,512]{2,1,0:T(8,128)(2,1)S(1)}, u32[]{:S(2)}, u32[]{:S(2)}) collective-permute-start(bf16[4,512,512]{2,1,0:T(8,128)(2,1)} %fusion.24), channel_id=1, source_target_pairs={{0,16},{1,17},{8,24},{9,25},{16,0},{17,1},{24,8},{25,9},{2,18},{3,... | collective-permute-start | bytes 6291464 | tf_op jit(solution)/shard_map/ppermute | solution.py:28
  69.1 47.9 %collective-permute-start.6 = (bf16[4,2048,128]{2,1,0:T(8,128)(2,1)}, bf16[4,2048,128]{2,1,0:T(8,128)(2,1)}, u32[]{:S(2)}, u32[]{:S(2)}) collective-permute-start(bf16[4,2048,128]{2,1,0:T(8,128)(2,1)} %pad_maximum_fusion.3), channel_id=1, source_target_pairs={{2,0},{4,2},{6,4},{3,1},{5,3},{7,5},{10,8},{12,10},{14,12},{11,9},... | collective-permute-start | bytes 6291464 | tf_op jit(solution)/shard_map/ppermute | solution.py:39
  70.3 47.5 %collective-permute-start.5 = (bf16[4,2048,128]{2,1,0:T(8,128)(2,1)}, bf16[4,2048,128]{2,1,0:T(8,128)(2,1)}, u32[]{:S(2)}, u32[]{:S(2)}) collective-permute-start(bf16[4,2048,128]{2,1,0:T(8,128)(2,1)} %pad_maximum_fusion.3), channel_id=1, source_target_pairs={{0,2},{2,4},{4,6},{1,3},{3,5},{5,7},{8,10},{10,12},{12,14},{9,11},... | collective-permute-start | bytes 6291464 | tf_op jit(solution)/shard_map/ppermute | solution.py:39
  117.8 46.7 %collective-permute-start.9 = (bf16[4,2048,128]{2,1,0:T(8,128)(2,1)}, bf16[4,2048,128]{2,1,0:T(8,128)(2,1)S(1)}, u32[]{:S(2)}, u32[]{:S(2)}) collective-permute-start(bf16[4,2048,128]{2,1,0:T(8,128)(2,1)} %collective-permute-done.5), channel_id=1, source_target_pairs={{0,2},{2,4},{4,6},{1,3},{3,5},{5,7},{8,10},{10,12},{12,14},{9,11},... | collective-permute-start | bytes 6291464 | tf_op jit(solution)/shard_map/ppermute | solution.py:39
  122.1 46.4 %collective-permute-start.10 = (bf16[4,2048,128]{2,1,0:T(8,128)(2,1)}, bf16[4,2048,128]{2,1,0:T(8,128)(2,1)}, u32[]{:S(2)}, u32[]{:S(2)}) collective-permute-start(bf16[4,2048,128]{2,1,0:T(8,128)(2,1)} %collective-permute-done.6), channel_id=1, source_target_pairs={{2,0},{4,2},{6,4},{3,1},{5,3},{7,5},{10,8},{12,10},{14,12},{11,9},... | collective-permute-start | bytes 6291464 | tf_op jit(solution)/shard_map/ppermute | solution.py:39
  124.6 52.8 %copy-start.23 = (s32[4]{0:T(128)S(1)}, s32[4]{0:T(128)}, u32[]{:S(2)}) copy-start(s32[4]{0:T(128)} %constant.209.clone) | copy-start | bytes 52
  124.7 54.0 %copy-start.22 = (s32[4]{0:T(128)S(1)}, s32[4]{0:T(128)}, u32[]{:S(2)}) copy-start(s32[4]{0:T(128)} %constant.206.clone) | copy-start | bytes 52
  124.7 55.3 %copy-start.21 = (s32[4]{0:T(128)S(1)}, s32[4]{0:T(128)}, u32[]{:S(2)}) copy-start(s32[4]{0:T(128)} %constant.203.clone) | copy-start | bytes 52
  124.7 56.4 %copy-start.19 = (f32[1024]{0:T(1024)S(1)}, f32[1024]{0:T(1024)}, u32[]{:S(2)}) copy-start(f32[1024]{0:T(1024)} %param.17) | copy-start | bytes 12292
  124.7 56.5 %copy-start.18 = (f32[16]{0:T(128)S(1)}, f32[16]{0:T(128)}, u32[]{:S(2)}) copy-start(f32[16]{0:T(128)} %param.16) | copy-start | bytes 196
  124.7 60.6 %collective-permute-start.11 = (bf16[4,512,512]{2,1,0:T(8,128)(2,1)}, bf16[4,512,512]{2,1,0:T(8,128)(2,1)}, u32[]{:S(2)}, u32[]{:S(2)}) collective-permute-start(bf16[4,512,512]{2,1,0:T(8,128)(2,1)} %fusion.24), channel_id=1, source_target_pairs={{0,17},{1,16},{8,25},{9,24},{16,1},{17,0},{24,9},{25,8},{2,19},{3,... | collective-permute-start | bytes 6291464 | tf_op jit(solution)/shard_map/ppermute | solution.py:28
  126.1 67.8 %collective-permute-start.14 = (bf16[4,2048,128]{2,1,0:T(8,128)(2,1)}, bf16[4,2048,128]{2,1,0:T(8,128)(2,1)}, u32[]{:S(2)}, u32[]{:S(2)}) collective-permute-start(bf16[4,2048,128]{2,1,0:T(8,128)(2,1)} %pad_maximum_fusion.3), channel_id=1, source_target_pairs={{0,8},{8,0},{16,24},{24,16},{1,9},{9,1},{17,25},{25,17},{2,10},{10... | collective-permute-start | bytes 6291464 | tf_op jit(solution)/shard_map/ppermute | solution.py:32
  173.6 20.3 %collective-permute-start.15 = (bf16[4,2048,128]{2,1,0:T(8,128)(2,1)S(1)}, bf16[4,2048,128]{2,1,0:T(8,128)(2,1)}, u32[]{:S(2)}, u32[]{:S(2)}) collective-permute-start(bf16[4,2048,128]{2,1,0:T(8,128)(2,1)S(1)} %get-tuple-element.75), channel_id=1, source_target_pairs={{0,8},{8,0},{16,24},{24,16},{1,9},{9,1},{17,25},{25,17},{2,10},{10... | collective-permute-start | bytes 6291464 | tf_op jit(solution)/shard_map/ppermute | solution.py:32
  177.5 16.5 %collective-permute-start.16 = (bf16[4,2048,128]{2,1,0:T(8,128)(2,1)}, bf16[4,2048,128]{2,1,0:T(8,128)(2,1)}, u32[]{:S(2)}, u32[]{:S(2)}) collective-permute-start(bf16[4,2048,128]{2,1,0:T(8,128)(2,1)} %get-tuple-element.76), channel_id=1, source_target_pairs={{0,8},{8,0},{16,24},{24,16},{1,9},{9,1},{17,25},{25,17},{2,10},{10... | collective-permute-start | bytes 6291464 | tf_op jit(solution)/shard_map/ppermute | solution.py:32
  181.3 3.5 copy-start.12
  186.7 48.5 %collective-permute-start.12 = (bf16[4,2048,128]{2,1,0:T(8,128)(2,1)S(1)}, bf16[4,2048,128]{2,1,0:T(8,128)(2,1)S(1)}, u32[]{:S(2)}, u32[]{:S(2)}) collective-permute-start(bf16[4,2048,128]{2,1,0:T(8,128)(2,1)S(1)} %copy-done.5), channel_id=1, source_target_pairs={{0,2},{2,4},{4,6},{1,3},{3,5},{5,7},{8,10},{10,12},{12,14},{9,11},... | collective-permute-start | bytes 6291464 | tf_op jit(solution)/shard_map/ppermute | solution.py:39
  190.9 48.6 %collective-permute-start.13 = (bf16[4,2048,128]{2,1,0:T(8,128)(2,1)}, bf16[4,2048,128]{2,1,0:T(8,128)(2,1)}, u32[]{:S(2)}, u32[]{:S(2)}) collective-permute-start(bf16[4,2048,128]{2,1,0:T(8,128)(2,1)} %collective-permute-done.10), channel_id=1, source_target_pairs={{2,0},{4,2},{6,4},{3,1},{5,3},{7,5},{10,8},{12,10},{14,12},{11,9},... | collective-permute-start | bytes 6291464 | tf_op jit(solution)/shard_map/ppermute | solution.py:39
  194.0 51.6 %copy-start.3 = (bf16[4,2048,512]{2,1,0:T(8,128)(2,1)}, bf16[4,2048,512]{2,1,0:T(8,128)(2,1)S(1)}, u32[]{:S(2)}) copy-start(bf16[4,2048,512]{2,1,0:T(8,128)(2,1)S(1)} %constant_dynamic-update-slice_fusion) | copy-start | bytes 25165828
  202.8 31.3 %copy-start.2 = (bf16[12,2048,256]{2,1,0:T(8,128)(2,1)}, bf16[12,2048,256]{2,1,0:T(8,128)(2,1)S(1)}, u32[]{:S(2)}) copy-start(bf16[12,2048,256]{2,1,0:T(8,128)(2,1)S(1)} %maximum_maximum_fusion) | copy-start | bytes 37748740
  239.5 9.4 %slice-start = ((s8[12582912]{0:T(1024)(128)(4,1)}), s8[4194304]{0:T(1024)(128)(4,1)S(1)}, s32[]{:S(2)}) async-start(s8[12582912]{0:T(1024)(128)(4,1)} %bitcast.115), calls=%async_computation | async-start | bytes 8388608
  239.5 9.4 %slice-start.1 = ((s8[12582912]{0:T(1024)(128)(4,1)}), s8[4194304]{0:T(1024)(128)(4,1)S(1)}, s32[]{:S(2)}) async-start(s8[12582912]{0:T(1024)(128)(4,1)} %bitcast.115), calls=%async_computation.1 | async-start | bytes 8388608
  241.9 38.5 %copy-start.13 = (bf16[4,2048,128]{2,1,0:T(8,128)(2,1)}, bf16[4,2048,128]{2,1,0:T(8,128)(2,1)S(1)}, u32[]{:S(2)}) copy-start(bf16[4,2048,128]{2,1,0:T(8,128)(2,1)S(1)} %select_select_fusion) | copy-start | bytes 6291460
  241.9 11.9 %collective-permute-start.17 = (bf16[4,2048,128]{2,1,0:T(8,128)(2,1)S(1)}, bf16[4,2048,128]{2,1,0:T(8,128)(2,1)S(1)}, u32[]{:S(2)}, u32[]{:S(2)}) collective-permute-start(bf16[4,2048,128]{2,1,0:T(8,128)(2,1)S(1)} %select_select_fusion), channel_id=1, source_target_pairs={{0,8},{8,0},{16,24},{24,16},{1,9},{9,1},{17,25},{25,17},{2,10},{10... | collective-permute-start | bytes 6291464 | tf_op jit(solution)/shard_map/ppermute | solution.py:32
  245.6 4.4 slice-start.2
  278.5 25.1 %collective-permute-start.18 = (bf16[2,512,512]{2,1,0:T(8,128)(2,1)}, bf16[2,512,512]{2,1,0:T(8,128)(2,1)S(1)}, u32[]{:S(2)}, u32[]{:S(2)}) collective-permute-start(bf16[2,512,512]{2,1,0:T(8,128)(2,1)} %bitcast.22), channel_id=1, source_target_pairs={{0,1},{1,0},{8,9},{9,8},{16,17},{17,16},{24,25},{25,24},{2,3},{3,2... | collective-permute-start | bytes 3145736 | tf_op jit(solution)/shard_map/ppermute | solution.py:28
  303.7 23.2 %collective-permute-start.21 = (bf16[2,512,512]{2,1,0:T(8,128)(2,1)}, bf16[2,512,512]{2,1,0:T(8,128)(2,1)S(1)}, u32[]{:S(2)}, u32[]{:S(2)}) collective-permute-start(bf16[2,512,512]{2,1,0:T(8,128)(2,1)} %bitcast.31), channel_id=1, source_target_pairs={{0,1},{1,0},{8,9},{9,8},{16,17},{17,16},{24,25},{25,24},{2,3},{3,2... | collective-permute-start | bytes 3145736 | tf_op jit(solution)/shard_map/ppermute | solution.py:28
  303.7 11.0 %copy-start.6 = (bf16[2,512,512]{2,1,0:T(8,128)(2,1)}, bf16[2,512,512]{2,1,0:T(8,128)(2,1)S(1)}, u32[]{:S(2)}) copy-start(bf16[2,512,512]{2,1,0:T(8,128)(2,1)S(1)} %collective-permute-done.18) | copy-start | bytes 3145732
  338.7 13.3 %copy-start.7 = (bf16[2,512,512]{2,1,0:T(8,128)(2,1)S(1)}, bf16[2,512,512]{2,1,0:T(8,128)(2,1)}, u32[]{:S(2)}) copy-start(bf16[2,512,512]{2,1,0:T(8,128)(2,1)} %copy-done.6) | copy-start | bytes 3145732
  350.4 5.4 %copy-start = (f32[1024,512]{1,0:T(8,128)S(1)}, f32[1024,512]{1,0:T(8,128)}, u32[]{:S(2)}) copy-start(f32[1024,512]{1,0:T(8,128)} %slice.130) | copy-start | bytes 6291460
  350.4 23.1 %collective-permute-start.27 = (bf16[2,512,512]{2,1,0:T(8,128)(2,1)S(1)}, bf16[2,512,512]{2,1,0:T(8,128)(2,1)S(1)}, u32[]{:S(2)}, u32[]{:S(2)}) collective-permute-start(bf16[2,512,512]{2,1,0:T(8,128)(2,1)S(1)} %bitcast.118), channel_id=1, source_target_pairs={{0,1},{1,0},{8,9},{9,8},{16,17},{17,16},{24,25},{25,24},{2,3},{3,2... | collective-permute-start | bytes 3145736 | tf_op jit(solution)/shard_map/ppermute | solution.py:28
  352.3 22.9 %collective-permute-start.19 = (bf16[2,512,512]{2,1,0:T(8,128)(2,1)S(1)}, bf16[2,512,512]{2,1,0:T(8,128)(2,1)S(1)}, u32[]{:S(2)}, u32[]{:S(2)}) collective-permute-start(bf16[2,512,512]{2,1,0:T(8,128)(2,1)S(1)} %fusion.33), channel_id=1, source_target_pairs={{0,16},{1,17},{8,24},{9,25},{16,0},{17,1},{24,8},{25,9},{2,18},{3,... | collective-permute-start | bytes 3145736 | tf_op jit(solution)/shard_map/ppermute | solution.py:28
  355.6 40.3 %collective-permute-start.24 = (bf16[2,512,512]{2,1,0:T(8,128)(2,1)S(1)}, bf16[2,512,512]{2,1,0:T(8,128)(2,1)S(1)}, u32[]{:S(2)}, u32[]{:S(2)}) collective-permute-start(bf16[2,512,512]{2,1,0:T(8,128)(2,1)S(1)} %bitcast.117), channel_id=1, source_target_pairs={{0,1},{1,0},{8,9},{9,8},{16,17},{17,16},{24,25},{25,24},{2,3},{3,2... | collective-permute-start | bytes 3145736 | tf_op jit(solution)/shard_map/ppermute | solution.py:28
  356.4 41.3 %collective-permute-start.22 = (bf16[2,512,512]{2,1,0:T(8,128)(2,1)S(1)}, bf16[2,512,512]{2,1,0:T(8,128)(2,1)S(1)}, u32[]{:S(2)}, u32[]{:S(2)}) collective-permute-start(bf16[2,512,512]{2,1,0:T(8,128)(2,1)S(1)} %fusion.34), channel_id=1, source_target_pairs={{0,16},{1,17},{8,24},{9,25},{16,0},{17,1},{24,8},{25,9},{2,18},{3,... | collective-permute-start | bytes 3145736 | tf_op jit(solution)/shard_map/ppermute | solution.py:28
  373.8 46.0 %collective-permute-start.28 = (bf16[2,512,512]{2,1,0:T(8,128)(2,1)S(1)}, bf16[2,512,512]{2,1,0:T(8,128)(2,1)S(1)}, u32[]{:S(2)}, u32[]{:S(2)}) collective-permute-start(bf16[2,512,512]{2,1,0:T(8,128)(2,1)S(1)} %fusion.36), channel_id=1, source_target_pairs={{0,16},{1,17},{8,24},{9,25},{16,0},{17,1},{24,8},{25,9},{2,18},{3,... | collective-permute-start | bytes 3145736 | tf_op jit(solution)/shard_map/ppermute | solution.py:28
  376.7 70.2 %collective-permute-start.20 = (bf16[2,512,512]{2,1,0:T(8,128)(2,1)}, bf16[2,512,512]{2,1,0:T(8,128)(2,1)}, u32[]{:S(2)}, u32[]{:S(2)}) collective-permute-start(bf16[2,512,512]{2,1,0:T(8,128)(2,1)} %add_convert_fusion.3), channel_id=1, source_target_pairs={{0,8},{8,0},{16,24},{24,16},{1,9},{9,1},{17,25},{25,17},{2,10},{10... | collective-permute-start | bytes 3145736 | tf_op jit(solution)/shard_map/ppermute | solution.py:32
  396.3 46.0 %collective-permute-start.25 = (bf16[2,512,512]{2,1,0:T(8,128)(2,1)S(1)}, bf16[2,512,512]{2,1,0:T(8,128)(2,1)S(1)}, u32[]{:S(2)}, u32[]{:S(2)}) collective-permute-start(bf16[2,512,512]{2,1,0:T(8,128)(2,1)S(1)} %fusion.35), channel_id=1, source_target_pairs={{0,16},{1,17},{8,24},{9,25},{16,0},{17,1},{24,8},{25,9},{2,18},{3,... | collective-permute-start | bytes 3145736 | tf_op jit(solution)/shard_map/ppermute | solution.py:28
  399.2 49.5 %collective-permute-start.23 = (bf16[2,512,512]{2,1,0:T(8,128)(2,1)}, bf16[2,512,512]{2,1,0:T(8,128)(2,1)}, u32[]{:S(2)}, u32[]{:S(2)}) collective-permute-start(bf16[2,512,512]{2,1,0:T(8,128)(2,1)} %add_convert_fusion.2), channel_id=1, source_target_pairs={{0,8},{8,0},{16,24},{24,16},{1,9},{9,1},{17,25},{25,17},{2,10},{10... | collective-permute-start | bytes 3145736 | tf_op jit(solution)/shard_map/ppermute | solution.py:32
  420.3 30.1 %collective-permute-start.29 = (bf16[2,512,512]{2,1,0:T(8,128)(2,1)S(1)}, bf16[2,512,512]{2,1,0:T(8,128)(2,1)}, u32[]{:S(2)}, u32[]{:S(2)}) collective-permute-start(bf16[2,512,512]{2,1,0:T(8,128)(2,1)S(1)} %add_convert_fusion), channel_id=1, source_target_pairs={{0,8},{8,0},{16,24},{24,16},{1,9},{9,1},{17,25},{25,17},{2,10},{10... | collective-permute-start | bytes 3145736 | tf_op jit(solution)/shard_map/ppermute | solution.py:32
  443.8 8.2 %collective-permute-start.26 = (bf16[2,512,512]{2,1,0:T(8,128)(2,1)}, bf16[2,512,512]{2,1,0:T(8,128)(2,1)S(1)}, u32[]{:S(2)}, u32[]{:S(2)}) collective-permute-start(bf16[2,512,512]{2,1,0:T(8,128)(2,1)} %add_convert_fusion.1), channel_id=1, source_target_pairs={{0,8},{8,0},{16,24},{24,16},{1,9},{9,1},{17,25},{25,17},{2,10},{10... | collective-permute-start | bytes 3145736 | tf_op jit(solution)/shard_map/ppermute | solution.py:32
  (11 other events, 22.6 us)
